TPU v7x, 1024 devices: a whole 4x4x32 slice. The times are simulated.
1024 devices in a mesh: clu: 32 (over y, x, core), mem: 32 (over z).
Axes of the slice: x: 4, y: 4, z: 32, core: 2. Of those that a mesh axis runs over, the one named last changes fastest.
Arguments:
- seed_class: int32 [262144], P(('clu', 'mem')), may hold values from 0 to 15
- seed_weight: float32 [262144], P(('clu', 'mem')), may hold values from 0.3 to 3
- tile_values: bfloat16 [32, 32, 96, 128, 128], P('clu', 'mem'), may hold values from 0 to 1
- tile_rows: int32 [32, 32, 96], P('clu', 'mem'), may hold values from 0 to 63
- tile_cols: int32 [32, 32, 96], P('clu', 'mem'), may hold values from 0 to 63
- tile_count: int32 [32, 32], P('clu', 'mem'), may hold values from 12 to 96, as said below
Outputs:
- scores: float32 [8, 262144], P(None, ('clu', 'mem'))
- residual: float32 [8, 262144], P(None, ('clu', 'mem'))
Inputs may be any that keep to these rules, and one draw needn't show every extreme that they name: `tile_count`: some device uses all 96 slots in every draw.
All inputs are finite; a program needn't handle non-finite values.
Results may differ from a plain program's by a relative error of at most 0.0027.
Values may be sent and summed in bfloat16 or wider, within the bound.
No kernel may reach another device: no remote copies, remote signals or barrier semaphores. Data moves between devices by JAX's collectives and lax.ppermute only.
A program may use at most 32 MiB of HBM per device.

v0:
```python
import jax
import jax.numpy as jnp
from jax import lax
from jax.sharding import PartitionSpec as P

CLASSES = 8
NB_DEV = 2
ITERS = 2


def spread(row_part, col_part):
    width = row_part.shape[0]
    from_rows = lax.psum_scatter(
        row_part.reshape(width, -1), "mem", scatter_dimension=1, tiled=True
    )
    from_cols = lax.psum_scatter(
        col_part.reshape(width, -1), "clu", scatter_dimension=1, tiled=True
    )
    return from_rows + from_cols


def squares(residual):
    return lax.psum(jnp.sum(residual * residual, axis=1), ("clu", "mem"))


def on_device(seed_class, seed_weight, tile_values, tile_rows, tile_cols, tile_count):
    tiles = tile_values[0, 0]
    rows = tile_rows[0, 0]
    cols = tile_cols[0, 0]
    count = tile_count[0, 0]
    slots = tiles.shape[0]
    side = tiles.shape[1]
    row_blocks = NB_DEV * lax.axis_size("mem")
    col_blocks = NB_DEV * lax.axis_size("clu")
    valid = (jnp.arange(slots, dtype=jnp.int32) < count).astype(jnp.float32)
    row_table = (rows[None, :] == jnp.arange(row_blocks, dtype=jnp.int32)[:, None]).astype(
        jnp.float32
    ) * valid[None, :]
    col_table = (cols[None, :] == jnp.arange(col_blocks, dtype=jnp.int32)[:, None]).astype(
        jnp.float32
    ) * valid[None, :]
    highest = lax.Precision.HIGHEST
    row_totals = jnp.sum(tiles, axis=2, dtype=jnp.float32)
    col_totals = jnp.sum(tiles, axis=1, dtype=jnp.float32)
    row_part = jnp.einsum("rt,ti->ri", row_table, row_totals, precision=highest)
    col_part = jnp.einsum("kt,tj->kj", col_table, col_totals, precision=highest)
    degree = 1.0 + spread(row_part[None], col_part[None])[0]
    inverse_root = lax.rsqrt(degree)
    classes_now = jnp.arange(CLASSES, dtype=jnp.int32)[:, None]
    labels = jnp.where(seed_class[None, :] == classes_now, seed_weight[None, :], jnp.float32(0.0))
    scores = jnp.zeros_like(labels)
    residual = labels
    direction = labels
    norm_now = squares(residual)
    for step in range(ITERS):
        width = direction.shape[0]
        scaled = (inverse_root[None, :] * direction).astype(jnp.bfloat16)
        col_panel = lax.all_gather(scaled, "clu", axis=1, tiled=True).reshape(
            width, col_blocks, side
        )
        row_panel = lax.all_gather(scaled, "mem", axis=1, tiled=True).reshape(
            width, row_blocks, side
        )
        forward = jnp.einsum(
            "tij,ctj->cti",
            tiles,
            jnp.take(col_panel, cols, axis=1),
            preferred_element_type=jnp.float32,
        )
        backward = jnp.einsum(
            "tij,cti->ctj",
            tiles,
            jnp.take(row_panel, rows, axis=1),
            preferred_element_type=jnp.float32,
        )
        row_sum = jnp.einsum("rt,cti->cri", row_table, forward, precision=highest)
        col_sum = jnp.einsum("kt,ctj->ckj", col_table, backward, precision=highest)
        image_sum = spread(row_sum, col_sum)
        image = direction - 0.99 * inverse_root[None, :] * image_sum
        alpha = norm_now / lax.psum(jnp.sum(direction * image, axis=1), ("clu", "mem"))
        scores = scores + alpha[:, None] * direction
        residual = residual - alpha[:, None] * image
        if step + 1 < ITERS:
            norm_next = squares(residual)
            direction = residual + (norm_next / norm_now)[:, None] * direction
            norm_now = norm_next
    return (scores, residual)


def solution(mesh):
    in_specs = (
        P(("clu", "mem")),
        P(("clu", "mem")),
        P("clu", "mem", None, None, None),
        P("clu", "mem", None),
        P("clu", "mem", None),
        P("clu", "mem"),
    )
    out_specs = (P(None, ("clu", "mem")), P(None, ("clu", "mem")))
    return jax.shard_map(
        on_device, mesh=mesh, in_specs=in_specs, out_specs=out_specs, check_vma=False
    )
```

profile of v0, /device:TPU:1, one launch (start us, length us, event | category | flops | bytes accessed | tf_op | source)
XLA Modules:
  0.0 1460.4 jit_solution(2782124359821547454)
XLA Ops:
  7.2 0.0 copy-start.3
  7.2 0.0 reduce-scatter.21.cloned.1.call-start
  7.9 2.8 convert_reduce_fusion
  10.7 0.0 copy-done.3
  10.7 0.2 fusion.32
  10.9 2.7 copy.14
  13.6 0.0 copy-start.4
  13.6 0.0 reduce-scatter.21.cloned.1.call-update
  13.6 0.0 reduce-scatter.19.cloned.1.call-start
  13.6 0.6 copy-done.4
  14.2 0.2 fusion.34
  14.4 2.6 copy.12
  17.0 0.0 copy-start.1
  17.0 0.0 copy-start.2
  17.0 0.0 copy-start
  17.0 0.0 reduce-scatter.19.cloned.1.call-update
  17.0 0.0 reduce-scatter.13.cloned.1.call-start
  17.2 139.1 %reduce-scatter.21.cloned.1.call-done = f32[256,1]{1,0:T(8,128)} async-done(((f32[8192,1]{1,0:T(8,128)}), f32[256,1]{1,0:T(8,128)}) %reduce-scatter.21.cloned.1.call-update) | async-done | bytes 1040
  156.3 1.0 copy.15
  157.3 125.7 %reduce-scatter.19.cloned.1.call-done = f32[256,1]{1,0:T(8,128)} async-done(((f32[8192,1]{1,0:T(8,128)}), f32[256,1]{1,0:T(8,128)}) %reduce-scatter.19.cloned.1.call-update) | async-done | bytes 1040
  283.0 1.0 copy.13
  284.0 0.0 copy-done.1
  284.0 0.0 copy-done.2
  284.0 40.3 %all_gather.13 = bf16[8,8192]{1,0:T(8,128)(2,1)S(1)} all-gather(bf16[8,256]{1,0:T(8,128)(2,1)S(1)} %fusion.55), channel_id=1, replica_groups=mesh['clu'=32,'mem'=32] {'mem'}, dimensions={1}, use_global_device_ids=true | all-gather | bytes 135168 | tf_op jit(solution)/shard_map/all_gather | solution.py:61
  324.4 58.9 %all_gather.12 = bf16[8,8192]{1,0:T(8,128)(2,1)S(1)} all-gather(bf16[8,256]{1,0:T(8,128)(2,1)S(1)} %fusion.55), channel_id=1, replica_groups=mesh['clu'=32,'mem'=32] {'clu'}, dimensions={1}, use_global_device_ids=true | all-gather | bytes 135168 | tf_op jit(solution)/shard_map/all_gather | solution.py:58
  383.2 1.3 gather_fusion.1
  384.6 0.0 copy-done
  384.6 1.9 fusion.4
  386.5 0.4 convolution_bitcast_fusion.2
  386.9 0.8 copy.42
  387.8 0.0 reduce-scatter.13.cloned.1.call-update
  387.8 0.0 reduce-scatter.11.cloned.1.call-start
  387.8 0.7 gather_fusion
  388.5 1.7 fusion.6
  390.2 0.5 convolution_bitcast_fusion.3
  390.7 0.9 copy.43
  391.6 0.0 reduce-scatter.11.cloned.1.call-update
  391.6 0.0 reduce-scatter.17.cloned.1.call-start
  391.6 119.7 %reduce-scatter.13.cloned.1.call-done = f32[8,256]{1,0:T(8,128)} async-done(((f32[8,8192]{1,0:T(8,128)}), f32[8,256]{1,0:T(8,128)}) %reduce-scatter.13.cloned.1.call-update) | async-done | bytes 8208 | tf_op jit(solution)/shard_map/reduce_scatter | solution.py:16
  511.3 113.9 %reduce-scatter.11.cloned.1.call-done = f32[8,256]{1,0:T(8,128)} async-done(((f32[8,8192]{1,0:T(8,128)}), f32[8,256]{1,0:T(8,128)}) %reduce-scatter.11.cloned.1.call-update) | async-done | bytes 8208 | tf_op jit(solution)/shard_map/reduce_scatter | solution.py:13
  625.2 0.9 fusion.56
  626.1 177.3 %all-reduce = (f32[8]{0:T(128)S(1)}, f32[8]{0:T(128)S(1)}) all-reduce(f32[8]{0:T(128)S(1)} %get-tuple-element.6, f32[8]{0:T(128)S(1)} %get-tuple-element.5), channel_id=1, replica_groups=mesh['clu'=32,'mem'=32] {'clu','mem'}, use_global_device_ids=true, to_apply=%region_1.0 | all-reduce | flops 16 | bytes 128 | tf_op jit(solution)/shard_map/psum | solution.py:23
  803.3 0.2 multiply_reduce_fusion.1
  803.5 153.4 %psum.30 = f32[8]{0:T(128)S(1)} all-reduce(f32[8]{0:T(128)S(1)} %multiply_reduce_fusion.1), channel_id=1, replica_groups=mesh['clu'=32,'mem'=32] {'clu','mem'}, use_global_device_ids=true, to_apply=%region_11.13 | all-reduce | flops 8 | bytes 64 | tf_op jit(solution)/shard_map/psum | solution.py:23
  956.9 0.1 multiply_convert_fusion
  957.0 39.4 %all_gather.15 = bf16[8,8192]{1,0:T(8,128)(2,1)S(1)} all-gather(bf16[8,256]{1,0:T(8,128)(2,1)S(1)} %multiply_convert_fusion), channel_id=1, replica_groups=mesh['clu'=32,'mem'=32] {'mem'}, dimensions={1}, use_global_device_ids=true | all-gather | bytes 135168 | tf_op jit(solution)/shard_map/all_gather | solution.py:61
  996.4 38.3 %all_gather.14 = bf16[8,8192]{1,0:T(8,128)(2,1)S(1)} all-gather(bf16[8,256]{1,0:T(8,128)(2,1)S(1)} %multiply_convert_fusion), channel_id=1, replica_groups=mesh['clu'=32,'mem'=32] {'clu'}, dimensions={1}, use_global_device_ids=true | all-gather | bytes 135168 | tf_op jit(solution)/shard_map/all_gather | solution.py:58
  1034.7 1.3 gather_fusion.3
  1036.0 0.7 gather_fusion.2
  1036.7 1.9 fusion
  1038.6 0.4 convolution_bitcast_fusion
  1039.0 0.8 copy.40
  1039.9 0.0 reduce-scatter.17.cloned.1.call-update
  1039.9 0.0 reduce-scatter.15.cloned.1.call-start
  1040.0 1.7 fusion.2
  1041.7 0.5 convolution_bitcast_fusion.1
  1042.2 0.9 copy.41
  1043.0 0.0 reduce-scatter.15.cloned.1.call-update
  1043.0 117.3 %reduce-scatter.17.cloned.1.call-done = f32[8,256]{1,0:T(8,128)} async-done(((f32[8,8192]{1,0:T(8,128)}), f32[8,256]{1,0:T(8,128)}) %reduce-scatter.17.cloned.1.call-update) | async-done | bytes 8208 | tf_op jit(solution)/shard_map/reduce_scatter | solution.py:16
  1160.3 113.4 %reduce-scatter.15.cloned.1.call-done = f32[8,256]{1,0:T(8,128)} async-done(((f32[8,8192]{1,0:T(8,128)}), f32[8,256]{1,0:T(8,128)}) %reduce-scatter.15.cloned.1.call-update) | async-done | bytes 8208 | tf_op jit(solution)/shard_map/reduce_scatter | solution.py:13
  1273.8 0.9 multiply_reduce_fusion
  1274.7 177.5 %psum.31 = f32[8]{0:T(128)S(1)} all-reduce(f32[8]{0:T(128)S(1)} %multiply_reduce_fusion), channel_id=1, replica_groups=mesh['clu'=32,'mem'=32] {'clu','mem'}, use_global_device_ids=true, to_apply=%region_15.17 | all-reduce | flops 8 | bytes 64 | tf_op jit(solution)/shard_map/psum | solution.py:80
  1452.2 1.4 multiply_subtract_fusion
  (12 shorter events, 0.1 us)
Async XLA Ops:
  7.2 3.6 copy-start.3
  7.2 149.1 %reduce-scatter.21.cloned.1.call-start = ((), (), s32[]{:S(2)}) async-start(), calls=%async_computation.11 | async-start | bytes 4325376
  13.6 0.7 copy-start.4
  13.6 269.4 %reduce-scatter.19.cloned.1.call-start = ((), (), s32[]{:S(2)}) async-start(), calls=%async_computation.10 | async-start | bytes 4325376
  17.0 267.0 %copy-start.1 = (f32[256]{0:T(256)S(1)}, f32[256]{0:T(256)}, u32[]{:S(2)}) copy-start(f32[256]{0:T(256)} %param.9) | copy-start | bytes 3076
  17.0 267.0 %copy-start.2 = (s32[256]{0:T(256)S(1)}, s32[256]{0:T(256)}, u32[]{:S(2)}) copy-start(s32[256]{0:T(256)} %param.8) | copy-start | bytes 3076
  17.0 367.5 %copy-start = (bf16[1,1,96,128,128]{4,3,2,1,0:T(8,128)(2,1)S(1)}, bf16[1,1,96,128,128]{4,3,2,1,0:T(8,128)(2,1)}, u32[]{:S(2)}) copy-start(bf16[1,1,96,128,128]{4,3,2,1,0:T(8,128)(2,1)} %param.10) | copy-start | bytes 9437188
  17.0 494.3 %reduce-scatter.13.cloned.1.call-start = ((), (), s32[]{:S(2)}) async-start(), calls=%async_computation.7 | async-start | bytes 270336 | tf_op jit(solution)/shard_map/reduce_scatter | solution.py:16
  387.8 237.4 %reduce-scatter.11.cloned.1.call-start = ((), (), s32[]{:S(2)}) async-start(), calls=%async_computation.6 | async-start | bytes 270336 | tf_op jit(solution)/shard_map/reduce_scatter | solution.py:13
  391.6 768.8 %reduce-scatter.17.cloned.1.call-start = ((), (), s32[]{:S(2)}) async-start(), calls=%async_computation.9 | async-start | bytes 270336 | tf_op jit(solution)/shard_map/reduce_scatter | solution.py:16
  1039.9 233.9 %reduce-scatter.15.cloned.1.call-start = ((), (), s32[]{:S(2)}) async-start(), calls=%async_computation.8 | async-start | bytes 270336 | tf_op jit(solution)/shard_map/reduce_scatter | solution.py:13
Sparse Core Ops, SparseCore 0:
  13.7 142.5 reduce-scatter.20
  160.1 122.8 reduce-scatter.18
  387.9 123.3 reduce-scatter.12
  514.9 110.2 reduce-scatter.10
  1040.0 120.2 reduce-scatter.16
  1163.6 110.1 reduce-scatter.14
where the time goes:
time: 1460 us
  waiting for transfers between devices  729 us (50%)
  blocking collectives  685 us (47%)
  local copies, waits for them, and re-layouts  15.2 us (1%)
  between operations  14.9 us (1%)
    psum x2, blocking collectives, squares(): return lax.psum(jnp.sum(residual * residual, axis=1), ('clu', 'mem'))  331 us
    unnamed x8, waiting for transfers between devices  265 us
    reduce_scatter x2, waiting for transfers between devices, spread(): lax.psum_scatter(col_part.reshape(width, -1), 'clu', scatter_dimension=1,...  237 us
    reduce_scatter x2, waiting for transfers between devices, spread(): lax.psum_scatter(row_part.reshape(width, -1), 'mem', scatter_dimension=1,...  227 us
    psum x1, blocking collectives, on_device(): lax.psum(jnp.sum(direction * image, axis=1), ('clu', 'mem'))  178 us
    all_gather x2, blocking collectives, on_device(): lax.all_gather(scaled, 'clu', axis=1, tiled=True)  97.1 us
    all_gather x2, blocking collectives, on_device(): lax.all_gather(scaled, 'mem', axis=1, tiled=True)  79.8 us
  transfers between devices with their start and end apart: 6, of which 6 were waited for; matrix products, arithmetic and copies ran while one was open for 1% of the time, Pallas kernels for 0%

commit v1 on v0

v1 whole, which is shorter than its diff:
```python
import jax
import jax.numpy as jnp
from jax import lax
from jax.sharding import PartitionSpec as P

CLASSES = 8
NB_DEV = 2
DAMP = 0.99
F32 = jnp.float32
BF16 = jnp.bfloat16
HIGHEST = lax.Precision.HIGHEST


def swap(parts, axis):
    return lax.all_to_all(parts, axis, 0, 0, tiled=True)


def gather(own, axis):
    size = lax.axis_size(axis)
    return swap(jnp.broadcast_to(own[None], (size,) + own.shape), axis)


def split3(x):
    high = lax.reduce_precision(x, 8, 7)
    rest = x - high
    mid = lax.reduce_precision(rest, 8, 7)
    return jnp.concatenate([high, mid, rest - mid]).astype(BF16)


def on_device(seed_class, seed_weight, tile_values, tile_rows, tile_cols, tile_count):
    tiles = tile_values[0, 0]
    rows = tile_rows[0, 0]
    cols = tile_cols[0, 0]
    count = tile_count[0, 0]
    slots, side = tiles.shape[0], tiles.shape[1]
    n_mem, n_clu = lax.axis_size("mem"), lax.axis_size("clu")
    row_blocks, col_blocks = NB_DEV * n_mem, NB_DEV * n_clu
    valid = (jnp.arange(slots, dtype=jnp.int32) < count).astype(F32)
    row_table = (rows[None, :] == jnp.arange(row_blocks, dtype=jnp.int32)[:, None]).astype(F32) * valid
    col_table = (cols[None, :] == jnp.arange(col_blocks, dtype=jnp.int32)[:, None]).astype(F32) * valid

    row_totals = jnp.sum(tiles, axis=2, dtype=F32)
    col_totals = jnp.sum(tiles, axis=1, dtype=F32)
    row_part = jnp.einsum("rt,ti->ri", row_table, row_totals, precision=HIGHEST)
    col_part = jnp.einsum("kt,tj->kj", col_table, col_totals, precision=HIGHEST)
    from_cols = swap(col_part.reshape(n_clu, 1, NB_DEV * side), "clu")
    from_rows = swap(row_part.reshape(n_mem, 1, NB_DEV * side), "mem")
    degree = 1.0 + jnp.sum(from_cols, axis=0) + jnp.sum(from_rows, axis=0)
    inverse_root = lax.rsqrt(degree).reshape(NB_DEV, side)

    kinds = seed_class.reshape(NB_DEV, side)
    weight = seed_weight.reshape(NB_DEV, side)
    own = jnp.concatenate([(inverse_root * weight).astype(BF16), kinds.astype(BF16)])
    row_own = gather(own, "mem")
    col_own = gather(own, "clu")
    classes_now = jnp.arange(CLASSES, dtype=jnp.int32)[:, None]

    def panel_of(gathered):
        value = gathered[:, :NB_DEV].reshape(-1, 1, side)
        kind = gathered[:, NB_DEV:].reshape(-1, 1, side)
        return jnp.where(kind == classes_now.astype(BF16), value, jnp.zeros((), BF16))

    labels = jnp.where(kinds[:, None] == classes_now, weight[:, None], jnp.float32(0.0))
    scale = inverse_root[:, None]

    def products(row_panel, col_panel):
        forward = jnp.einsum(
            "tij,tcj->tci", tiles, jnp.take(col_panel, cols, axis=0), preferred_element_type=F32
        )
        backward = jnp.einsum(
            "tij,tci->tcj", tiles, jnp.take(row_panel, rows, axis=0), preferred_element_type=F32
        )
        row_sum = jnp.einsum("rt,tci->rci", row_table, forward, precision=HIGHEST)
        col_sum = jnp.einsum("kt,tcj->kcj", col_table, backward, precision=HIGHEST)
        return row_sum, col_sum

    height = NB_DEV * CLASSES
    row_sum, col_sum = products(panel_of(row_own), panel_of(col_own))
    from_cols = jnp.sum(swap(col_sum.reshape(n_clu, height, side), "clu"), axis=0)
    from_rows = jnp.sum(swap(row_sum.astype(BF16).reshape(n_mem, height, side), "mem").astype(F32), axis=0)
    first = scale * (from_cols + from_rows).reshape(NB_DEV, CLASSES, side)

    scaled = scale * first
    col_scaled = gather(scaled.reshape(height, side), "clu").reshape(col_blocks, CLASSES, side)
    row_scaled = gather(scaled.astype(BF16).reshape(height, side), "mem").reshape(row_blocks, CLASSES, side)
    row_sum, col_sum = products(row_scaled, col_scaled.astype(BF16))
    moments = jnp.concatenate(
        [
            jnp.sum(labels * labels, axis=(0, 2)),
            jnp.sum(labels * first, axis=(0, 2)),
            jnp.sum(first * first, axis=(0, 2)),
            2.0 * jnp.sum(col_scaled * col_sum, axis=(0, 2)),
        ]
    )
    pieces = split3(moments)
    extra = jnp.zeros((8, side), BF16).at[0, : pieces.shape[0]].set(pieces)
    sent = jnp.concatenate(
        [
            row_sum.astype(BF16).reshape(n_mem, height, side),
            jnp.broadcast_to(extra[None], (n_mem, 8, side)),
        ],
        axis=1,
    )
    got = jnp.sum(swap(sent, "mem").astype(F32), axis=0)
    from_rows = got[:height]
    line = got[height:]
    sent = jnp.concatenate(
        [col_sum.reshape(n_clu, height, side), jnp.broadcast_to(line[None], (n_clu, 8, side))], axis=1
    )
    got = jnp.sum(swap(sent, "clu"), axis=0)
    second = scale * (got[:height] + from_rows).reshape(NB_DEV, CLASSES, side)
    m = got[height, : pieces.shape[0]].reshape(3, 4, CLASSES)
    m0, m1, m2, m3 = (m[0] + m[1] + m[2])[:, :, None]

    ratio = m1 / m0
    qq = m2 - ratio * m1
    q_image = m3 - ratio * (2.0 * qq + ratio * m1)
    alpha0 = m0 / (m0 - DAMP * m1)
    pace = DAMP * alpha0
    beta = pace * pace * qq / m0
    alpha1 = qq / (qq - DAMP * q_image - DAMP * pace * qq * (qq / m0))
    q = first - ratio * labels
    q_applied = q - DAMP * (second - ratio * first)
    direction = pace * q + beta * labels
    applied = pace * q_applied + beta * (labels - DAMP * first)
    scores = alpha0 * labels + alpha1 * direction
    residual = pace * q - alpha1 * applied

    def out(x):
        return jnp.swapaxes(x, 0, 1).reshape(CLASSES, NB_DEV * side)

    return (out(scores), out(residual))


def solution(mesh):
    in_specs = (
        P(("clu", "mem")),
        P(("clu", "mem")),
        P("clu", "mem", None, None, None),
        P("clu", "mem", None),
        P("clu", "mem", None),
        P("clu", "mem"),
    )
    out_specs = (P(None, ("clu", "mem")), P(None, ("clu", "mem")))
    return jax.shard_map(
        on_device, mesh=mesh, in_specs=in_specs, out_specs=out_specs, check_vma=False
    )
```

time: 1460 us -> 282 us (0.19)
  blocking collectives: 685 us -> 31.9 us
  waiting for transfers between devices: 729 us -> 152 us
  starting transfers between devices: 0.25 us -> 64.1 us
    psum x3 -> x0, blocking collectives: 508 us -> none  [the longest x2 331 us: squares(): return lax.psum(jnp.sum(residual * residual, axis=1), ('clu', 'mem'))]
    reduce_scatter x4 -> x0, waiting for transfers between devices: 464 us -> none  [the longest x2 237 us: spread(): lax.psum_scatter(col_part.reshape(width, -1), 'clu', scatter_dimension=1,...]
    unnamed x8 -> x0, waiting for transfers between devices: 265 us -> none
    all_gather x4 -> x0, blocking collectives: 177 us -> none  [the longest x2 97.1 us: on_device(): lax.all_gather(scaled, 'clu', axis=1, tiled=True)]
    all_to_all x0 -> x8, waiting for transfers between devices: none -> 152 us  [swap(): return lax.all_to_all(parts, axis, 0, 0, tiled=True)]
    all_to_all x0 -> x8, starting transfers between devices: none -> 64.1 us  [swap(): return lax.all_to_all(parts, axis, 0, 0, tiled=True)]
    all_to_all x0 -> x2, blocking collectives: none -> 31.9 us  [swap(): return lax.all_to_all(parts, axis, 0, 0, tiled=True)]
  transfers between devices with their start and end apart: 6 -> 8, of which waited for: 6 -> 8; matrix products, arithmetic and copies ran while one was open for 1% -> 4% of each run, Pallas kernels for 0% -> 0%
where the time goes in v1:
time: 282 us; the launch traced here: 281 us
  waiting for transfers between devices  152 us (54%)
  starting transfers between devices  64.1 us (23%)
  blocking collectives  31.9 us (11%)
  matrix products  13.4 us (5%)
  local copies, waits for them, and re-layouts  9.76 us (3%)
  other arithmetic  8.53 us (3%)
    all_to_all x8, waiting for transfers between devices, swap(): return lax.all_to_all(parts, axis, 0, 0, tiled=True)  152 us
    all_to_all x8, starting transfers between devices, swap(): return lax.all_to_all(parts, axis, 0, 0, tiled=True)  64.1 us
    all_to_all x2, blocking collectives, swap(): return lax.all_to_all(parts, axis, 0, 0, tiled=True)  31.9 us
  transfers between devices with their start and end apart: 8, of which 8 were waited for; matrix products, arithmetic and copies ran while one was open for 4% of the time, Pallas kernels for 0%

profile of v1, /device:TPU:1, one launch (start us, length us, event | category | flops | bytes accessed | tf_op | source)
XLA Modules:
  0.0 281.1 jit_solution(4133817040294905248)
XLA Ops:
  0.6 0.0 copy-start.8
  0.7 0.0 copy-start.10
  0.7 0.0 copy-start.11
  0.7 0.0 copy-start.4
  0.7 3.0 %convert_reduce_fusion.1 = (f32[96,128]{1,0:T(8,128)S(1)}, f32[96,128]{1,0:T(8,128)S(1)}) fusion(bf16[1,1,96,128,128]{4,3,2,1,0:T(8,128)(2,1)} %param.12), kind=kLoop, calls=%fused_computation.5 | loop fusion | flops 4694016 | bytes 3244032 | tf_op jit(solution)/shard_map/reduce_sum | solution.py:43
  4.4 0.8 fusion.29
  5.1 17.6 %all-to-all-start = ((f32[32,1,256]{2,1,0:T(1,128)}), f32[32,1,256]{2,1,0:T(1,128)S(1)}, u32[]{:S(2)}, u32[]{:S(2)}) async-start(f32[32,1,256]{2,1,0:T(1,128)} %bitcast.5), calls=%async_computation | async-start | bytes 65536 | tf_op jit(solution)/shard_map/all_to_all | solution.py:15
  22.8 0.0 copy-done.10
  22.8 0.8 fusion.27
  23.6 6.5 %all-to-all-done = f32[32,1,256]{2,1,0:T(1,128)S(1)} async-done(((f32[32,1,256]{2,1,0:T(1,128)}), f32[32,1,256]{2,1,0:T(1,128)S(1)}, u32[]{:S(2)}, u32[]{:S(2)}) %all-to-all-start) | async-done | bytes 32800 | tf_op jit(solution)/shard_map/all_to_all | solution.py:15
  30.1 19.3 %all-to-all-start.1 = ((f32[32,1,256]{2,1,0:T(1,128)}), f32[32,1,256]{2,1,0:T(1,128)S(1)}, u32[]{:S(2)}, u32[]{:S(2)}) async-start(f32[32,1,256]{2,1,0:T(1,128)} %bitcast.6), calls=%async_computation.1 | async-start | bytes 65536 | tf_op jit(solution)/shard_map/all_to_all | solution.py:15
  49.5 0.0 copy-start.6
  49.5 0.1 reduce_sum.109
  49.5 21.9 %all-to-all-done.1 = f32[32,1,256]{2,1,0:T(1,128)S(1)} async-done(((f32[32,1,256]{2,1,0:T(1,128)}), f32[32,1,256]{2,1,0:T(1,128)S(1)}, u32[]{:S(2)}, u32[]{:S(2)}) %all-to-all-start.1) | async-done | bytes 32800 | tf_op jit(solution)/shard_map/all_to_all | solution.py:15
  71.4 0.1 reduce_sum.111
  71.5 0.6 multiply_convert_fusion
  72.1 0.6 broadcast_in_dim.53
  72.7 5.6 %all-to-all-start.4 = ((bf16[32,4,128]{2,1,0:T(4,128)(2,1)}), bf16[32,4,128]{2,1,0:T(4,128)(2,1)S(1)}, u32[]{:S(2)}, u32[]{:S(2)}) async-start(bf16[32,4,128]{2,1,0:T(4,128)(2,1)} %broadcast_in_dim.53), calls=%async_computation.4 | async-start | bytes 65536 | tf_op jit(solution)/shard_map/all_to_all | solution.py:15
  78.3 0.0 copy-start.7
  78.3 7.3 %all-to-all-done.4 = bf16[32,4,128]{2,1,0:T(4,128)(2,1)S(1)} async-done(((bf16[32,4,128]{2,1,0:T(4,128)(2,1)}), bf16[32,4,128]{2,1,0:T(4,128)(2,1)S(1)}, u32[]{:S(2)}, u32[]{:S(2)}) %all-to-all-start.4) | async-done | bytes 32800 | tf_op jit(solution)/shard_map/all_to_all | solution.py:15
  85.7 3.8 %all-to-all-start.2 = ((bf16[32,4,128]{2,1,0:T(4,128)(2,1)}), bf16[32,4,128]{2,1,0:T(4,128)(2,1)S(1)}, u32[]{:S(2)}, u32[]{:S(2)}) async-start(bf16[32,4,128]{2,1,0:T(4,128)(2,1)} %broadcast_in_dim.53), calls=%async_computation.2 | async-start | bytes 65536 | tf_op jit(solution)/shard_map/all_to_all | solution.py:15
  89.6 22.0 %all-to-all-done.2 = bf16[32,4,128]{2,1,0:T(4,128)(2,1)S(1)} async-done(((bf16[32,4,128]{2,1,0:T(4,128)(2,1)}), bf16[32,4,128]{2,1,0:T(4,128)(2,1)S(1)}, u32[]{:S(2)}, u32[]{:S(2)}) %all-to-all-start.2) | async-done | bytes 32800 | tf_op jit(solution)/shard_map/all_to_all | solution.py:15
  111.6 0.1 compare_select_fusion
  111.7 1.3 gather_fusion
  113.0 0.0 copy-done
  113.0 1.9 fusion.6
  114.9 0.5 fusion.12
  115.4 0.8 copy.16
  116.2 0.0 copy-done.13
  116.2 5.5 %all-to-all-start.3 = ((f32[32,16,128]{2,1,0:T(8,128)}), f32[32,16,128]{2,1,0:T(8,128)S(1)}, u32[]{:S(2)}, u32[]{:S(2)}) async-start(f32[32,16,128]{2,1,0:T(8,128)} %bitcast.138), calls=%async_computation.3 | async-start | bytes 524288 | tf_op jit(solution)/shard_map/all_to_all | solution.py:15
  121.8 1.3 gather_fusion.1
  123.1 2.7 fusion.4
  125.8 0.5 convolution_convert_fusion.1
  126.3 0.7 copy.18
  127.0 3.8 %all-to-all-done.3 = f32[32,16,128]{2,1,0:T(8,128)S(1)} async-done(((f32[32,16,128]{2,1,0:T(8,128)}), f32[32,16,128]{2,1,0:T(8,128)S(1)}, u32[]{:S(2)}, u32[]{:S(2)}) %all-to-all-start.3) | async-done | bytes 262176 | tf_op jit(solution)/shard_map/all_to_all | solution.py:15
  130.8 3.8 %all-to-all-start.5 = ((bf16[32,16,128]{2,1,0:T(8,128)(2,1)}), bf16[32,16,128]{2,1,0:T(8,128)(2,1)S(1)}, u32[]{:S(2)}, u32[]{:S(2)}) async-start(bf16[32,16,128]{2,1,0:T(8,128)(2,1)} %bitcast.17), calls=%async_computation.5 | async-start | bytes 262144 | tf_op jit(solution)/shard_map/all_to_all | solution.py:15
  134.7 31.0 %all-to-all-done.5 = bf16[32,16,128]{2,1,0:T(8,128)(2,1)S(1)} async-done(((bf16[32,16,128]{2,1,0:T(8,128)(2,1)}), bf16[32,16,128]{2,1,0:T(8,128)(2,1)S(1)}, u32[]{:S(2)}, u32[]{:S(2)}) %all-to-all-start.5) | async-done | bytes 131104 | tf_op jit(solution)/shard_map/all_to_all | solution.py:15
  165.7 1.4 fusion.50
  167.1 0.7 fusion.96
  167.8 13.6 %all_to_all.50 = f32[32,16,128]{2,1,0:T(8,128)S(1)} all-to-all(f32[32,16,128]{2,1,0:T(8,128)S(1)} %broadcast_in_dim.60), channel_id=1, replica_groups=mesh['clu'=32,'mem'=32] {'clu'}, dimensions={0} | all-to-all | bytes 524288 | tf_op jit(solution)/shard_map/all_to_all | solution.py:15
  181.3 0.7 broadcast_in_dim.59
  182.0 4.6 %all-to-all-start.6 = ((bf16[32,16,128]{2,1,0:T(8,128)(2,1)}), bf16[32,16,128]{2,1,0:T(8,128)(2,1)}, u32[]{:S(2)}, u32[]{:S(2)}) async-start(bf16[32,16,128]{2,1,0:T(8,128)(2,1)} %broadcast_in_dim.59), calls=%async_computation.6 | async-start | bytes 262144 | tf_op jit(solution)/shard_map/all_to_all | solution.py:15
  186.6 1.4 gather_fusion.3
  188.1 2.7 fusion
  190.7 1.2 convolution_convert_fusion
  192.0 0.1 copy.22
  192.1 25.2 %all-to-all-done.6 = bf16[32,16,128]{2,1,0:T(8,128)(2,1)} async-done(((bf16[32,16,128]{2,1,0:T(8,128)(2,1)}), bf16[32,16,128]{2,1,0:T(8,128)(2,1)}, u32[]{:S(2)}, u32[]{:S(2)}) %all-to-all-start.6) | async-done | bytes 131104 | tf_op jit(solution)/shard_map/all_to_all | solution.py:15
  217.3 2.3 gather_fusion.2
  219.6 1.9 fusion.2
  221.6 0.0 copy-start.5
  221.6 0.0 copy-start.12
  221.6 0.6 fusion.14
  222.2 0.7 fusion.77
  222.9 0.1 fusion.76
  223.0 0.7 pad_maximum_fusion.1
  223.7 3.9 %all-to-all-start.8 = ((bf16[32,24,128]{2,1,0:T(8,128)(2,1)}), bf16[32,24,128]{2,1,0:T(8,128)(2,1)S(1)}, u32[]{:S(2)}, u32[]{:S(2)}) async-start(bf16[32,24,128]{2,1,0:T(8,128)(2,1)} %pad_maximum_fusion.1), calls=%async_computation.8 | async-start | bytes 393216 | tf_op jit(solution)/shard_map/all_to_all | solution.py:15
  227.6 0.2 copy.20
  227.7 34.0 %all-to-all-done.8 = bf16[32,24,128]{2,1,0:T(8,128)(2,1)S(1)} async-done(((bf16[32,24,128]{2,1,0:T(8,128)(2,1)}), bf16[32,24,128]{2,1,0:T(8,128)(2,1)S(1)}, u32[]{:S(2)}, u32[]{:S(2)}) %all-to-all-start.8) | async-done | bytes 196640 | tf_op jit(solution)/shard_map/all_to_all | solution.py:15
  261.8 18.3 %all_to_all.51 = f32[32,24,128]{2,1,0:T(8,128)S(1)} all-to-all(f32[32,24,128]{2,1,0:T(8,128)S(1)} %pad_maximum_fusion), channel_id=1, replica_groups=mesh['clu'=32,'mem'=32] {'clu'}, dimensions={0} | all-to-all | bytes 786432 | tf_op jit(solution)/shard_map/all_to_all | solution.py:15
  280.2 0.1 slice_add_fusion.1
  280.3 0.1 fusion.84
  280.4 0.1 broadcast_multiply_fusion
  280.4 0.0 copy-done.12
  280.5 0.7 fusion.60
  (42 shorter events, 0.4 us)
Async XLA Ops:
  0.6 112.4 %copy-start = (bf16[1,1,96,128,128]{4,3,2,1,0:T(8,128)(2,1)S(1)}, bf16[1,1,96,128,128]{4,3,2,1,0:T(8,128)(2,1)}, u32[]{:S(2)}) copy-start(bf16[1,1,96,128,128]{4,3,2,1,0:T(8,128)(2,1)} %param.12) | copy-start | bytes 9437188
  0.6 3.7 %copy-start.8 = (s32[1,1,96]{2,1,0:T(1,128)S(1)}, s32[1,1,96]{2,1,0:T(1,128)}, u32[]{:S(2)}) copy-start(s32[1,1,96]{2,1,0:T(1,128)} %param.14) | copy-start | bytes 1156
  0.7 22.1 %copy-start.10 = (s32[1,1,96]{2,1,0:T(1,128)S(1)}, s32[1,1,96]{2,1,0:T(1,128)}, u32[]{:S(2)}) copy-start(s32[1,1,96]{2,1,0:T(1,128)} %param.13) | copy-start | bytes 1156
  0.7 48.8 %copy-start.11 = (s32[256]{0:T(256)S(1)}, s32[256]{0:T(256)}, u32[]{:S(2)}) copy-start(s32[256]{0:T(256)} %param.10) | copy-start | bytes 3076
  0.7 70.8 %copy-start.4 = (f32[256]{0:T(256)S(1)}, f32[256]{0:T(256)}, u32[]{:S(2)}) copy-start(f32[256]{0:T(256)} %param.11) | copy-start | bytes 3076
  4.3 121.4 %copy-start.1 = (f32[96]{0:T(128)}, f32[96]{0:T(128)S(1)}, u32[]{:S(2)}) copy-start(f32[96]{0:T(128)S(1)} %compare_convert_fusion) | copy-start | bytes 1156
  5.1 25.0 %all-to-all-start = ((f32[32,1,256]{2,1,0:T(1,128)}), f32[32,1,256]{2,1,0:T(1,128)S(1)}, u32[]{:S(2)}, u32[]{:S(2)}) async-start(f32[32,1,256]{2,1,0:T(1,128)} %bitcast.5), calls=%async_computation | async-start | bytes 65536 | tf_op jit(solution)/shard_map/all_to_all | solution.py:15
  22.8 93.4 %copy-start.13 = (pred[96]{0:T(512)(128)(4,1)}, pred[96]{0:T(512)(128)(4,1)S(1)}, u32[]{:S(2)}) copy-start(pred[96]{0:T(512)(128)(4,1)S(1)} %compare_and_fusion) | copy-start | bytes 292
  23.6 99.5 %copy-start.14 = (pred[96]{0:T(512)(128)(4,1)}, pred[96]{0:T(512)(128)(4,1)S(1)}, u32[]{:S(2)}) copy-start(pred[96]{0:T(512)(128)(4,1)S(1)} %compare_and_fusion.1) | copy-start | bytes 292
  30.1 41.3 %all-to-all-start.1 = ((f32[32,1,256]{2,1,0:T(1,128)}), f32[32,1,256]{2,1,0:T(1,128)S(1)}, u32[]{:S(2)}, u32[]{:S(2)}) async-start(f32[32,1,256]{2,1,0:T(1,128)} %bitcast.6), calls=%async_computation.1 | async-start | bytes 65536 | tf_op jit(solution)/shard_map/all_to_all | solution.py:15
  49.5 66.8 %copy-start.6 = (s32[1024]{0:T(1024)}, s32[1024]{0:T(1024)S(1)}, u32[]{:S(2)}) copy-start(s32[1024]{0:T(1024)S(1)} %pad_clamp_fusion.1) | copy-start | bytes 12292
  72.7 13.0 %all-to-all-start.4 = ((bf16[32,4,128]{2,1,0:T(4,128)(2,1)}), bf16[32,4,128]{2,1,0:T(4,128)(2,1)S(1)}, u32[]{:S(2)}, u32[]{:S(2)}) async-start(bf16[32,4,128]{2,1,0:T(4,128)(2,1)} %broadcast_in_dim.53), calls=%async_computation.4 | async-start | bytes 65536 | tf_op jit(solution)/shard_map/all_to_all | solution.py:15
  78.3 43.4 %copy-start.7 = (s32[1024]{0:T(1024)}, s32[1024]{0:T(1024)S(1)}, u32[]{:S(2)}) copy-start(s32[1024]{0:T(1024)S(1)} %pad_clamp_fusion) | copy-start | bytes 12292
  85.7 25.9 %all-to-all-start.2 = ((bf16[32,4,128]{2,1,0:T(4,128)(2,1)}), bf16[32,4,128]{2,1,0:T(4,128)(2,1)S(1)}, u32[]{:S(2)}, u32[]{:S(2)}) async-start(bf16[32,4,128]{2,1,0:T(4,128)(2,1)} %broadcast_in_dim.53), calls=%async_computation.2 | async-start | bytes 65536 | tf_op jit(solution)/shard_map/all_to_all | solution.py:15
  116.2 14.5 %all-to-all-start.3 = ((f32[32,16,128]{2,1,0:T(8,128)}), f32[32,16,128]{2,1,0:T(8,128)S(1)}, u32[]{:S(2)}, u32[]{:S(2)}) async-start(f32[32,16,128]{2,1,0:T(8,128)} %bitcast.138), calls=%async_computation.3 | async-start | bytes 524288 | tf_op jit(solution)/shard_map/all_to_all | solution.py:15
  130.8 34.9 %all-to-all-start.5 = ((bf16[32,16,128]{2,1,0:T(8,128)(2,1)}), bf16[32,16,128]{2,1,0:T(8,128)(2,1)S(1)}, u32[]{:S(2)}, u32[]{:S(2)}) async-start(bf16[32,16,128]{2,1,0:T(8,128)(2,1)} %bitcast.17), calls=%async_computation.5 | async-start | bytes 262144 | tf_op jit(solution)/shard_map/all_to_all | solution.py:15
  182.0 35.3 %all-to-all-start.6 = ((bf16[32,16,128]{2,1,0:T(8,128)(2,1)}), bf16[32,16,128]{2,1,0:T(8,128)(2,1)}, u32[]{:S(2)}, u32[]{:S(2)}) async-start(bf16[32,16,128]{2,1,0:T(8,128)(2,1)} %broadcast_in_dim.59), calls=%async_computation.6 | async-start | bytes 262144 | tf_op jit(solution)/shard_map/all_to_all | solution.py:15
  190.7 30.8 %copy-start.2 = (f32[96]{0:T(128)S(1)}, f32[96]{0:T(128)}, u32[]{:S(2)}) copy-start(f32[96]{0:T(128)} %copy-done.1) | copy-start | bytes 1156
  190.7 30.8 %copy-start.9 = (s32[1,1,96]{2,1,0:T(1,128)S(1)}, s32[1,1,96]{2,1,0:T(1,128)}, u32[]{:S(2)}) copy-start(s32[1,1,96]{2,1,0:T(1,128)} %param.14) | copy-start | bytes 1156
  221.5 58.9 %copy-start.3 = (f32[2,128]{1,0:T(2,128)S(1)}, f32[2,128]{1,0:T(2,128)}, u32[]{:S(2)}) copy-start(f32[2,128]{1,0:T(2,128)} %get-tuple-element.29) | copy-start | bytes 3076
  221.6 58.9 %copy-start.5 = (f32[256]{0:T(256)S(1)}, f32[256]{0:T(256)}, u32[]{:S(2)}) copy-start(f32[256]{0:T(256)} %param.11) | copy-start | bytes 3076
  221.6 58.9 %copy-start.12 = (s32[256]{0:T(256)S(1)}, s32[256]{0:T(256)}, u32[]{:S(2)}) copy-start(s32[256]{0:T(256)} %param.10) | copy-start | bytes 3076
  223.7 38.0 %all-to-all-start.8 = ((bf16[32,24,128]{2,1,0:T(8,128)(2,1)}), bf16[32,24,128]{2,1,0:T(8,128)(2,1)S(1)}, u32[]{:S(2)}, u32[]{:S(2)}) async-start(bf16[32,24,128]{2,1,0:T(8,128)(2,1)} %pad_maximum_fusion.1), calls=%async_computation.8 | async-start | bytes 393216 | tf_op jit(solution)/shard_map/all_to_all | solution.py:15

commit v2 on v1

v2 whole, which is shorter than its diff:
```python
import functools

import jax
import jax.numpy as jnp
from jax import lax
from jax.experimental import pallas as pl
from jax.experimental.pallas import tpu as pltpu
from jax.sharding import PartitionSpec as P

CLASSES = 8
NB_DEV = 2
DAMP = 0.99
F32 = jnp.float32
BF16 = jnp.bfloat16
STEP = 16
LIMIT = 8


def swap(parts, axis):
    return lax.all_to_all(parts, axis, 0, 0, tiled=True)


def gather_both(sent):
    n_mem, n_clu = lax.axis_size("mem"), lax.axis_size("clu")
    from_clu = swap(sent[:n_clu], "clu")
    sent, from_clu = lax.optimization_barrier((sent, from_clu))
    return from_clu, swap(sent[:n_mem], "mem")


def split3(x):
    high = lax.reduce_precision(x, 8, 7)
    rest = x - high
    mid = lax.reduce_precision(rest, 8, 7)
    return jnp.concatenate([high, mid, rest - mid]).astype(BF16)


def sum_slots(slots_ref, count_ref, tiles_ref, acc, left_of, side):
    step = pl.program_id(0)
    into = slots_ref

    @pl.when(step == 0)
    def _():
        acc[...] = jnp.zeros_like(acc)

    for t in range(STEP):
        slot = step * STEP + t
        block = into[slot]
        used = jnp.where(slot < count_ref[0], 1.0, 0.0)
        product = lax.dot_general(
            left_of(slot), tiles_ref[t], (((1,), (side,)), ((), ())), preferred_element_type=F32
        )
        acc[block] += used * product


def totals_kernel(side, into_ref, count_ref, tiles_ref, out, acc):
    ones = jnp.ones((CLASSES, tiles_ref.shape[2]), BF16)
    sum_slots(into_ref, count_ref, tiles_ref, acc, lambda slot: ones, side)

    @pl.when(pl.program_id(0) == pl.num_programs(0) - 1)
    def _():
        out[...] = acc[:, 0, :]


def products_kernel(side, into_ref, count_ref, from_ref, panel, tiles_ref, out, acc, wide):
    @pl.when(pl.program_id(0) == 0)
    def _():
        wide[...] = panel[...].astype(F32).reshape(wide.shape)

    sum_slots(
        into_ref, count_ref, tiles_ref, acc, lambda slot: wide[from_ref[slot]].astype(BF16), side
    )

    @pl.when(pl.program_id(0) == pl.num_programs(0) - 1)
    def _():
        out[...] = acc[...].reshape(out.shape).astype(out.dtype)


def middle_kernel(from_cols, from_rows, scale, first, sent):
    scale = scale[...]
    image = jnp.sum(from_cols[...].astype(F32), axis=0) + jnp.sum(from_rows[...].astype(F32), axis=0)
    image = scale * image
    first[...] = image
    sent[...] = jnp.broadcast_to((scale * image).astype(BF16)[None], sent.shape)


def call_on_tiles(kernel, index, panels, tiles, out, scratch, limit):
    slots, side = tiles.shape[0], tiles.shape[1]

    def whole(x):
        return pl.BlockSpec(x.shape, lambda i, *_: (0,) * len(x.shape))

    return pl.pallas_call(
        kernel,
        grid_spec=pltpu.PrefetchScalarGridSpec(
            num_scalar_prefetch=len(index),
            grid=(slots // STEP,),
            in_specs=[whole(p) for p in panels]
            + [pl.BlockSpec((STEP, side, side), lambda i, *_: (i, 0, 0))],
            out_specs=whole(out),
            scratch_shapes=[pltpu.VMEM(x, F32) for x in scratch],
        ),
        out_shape=out,
        compiler_params=pltpu.CompilerParams(
            dimension_semantics=("arbitrary",), vmem_limit_bytes=limit << 20
        ),
        cost_estimate=pl.CostEstimate(
            flops=2 * CLASSES * slots * side * side,
            bytes_accessed=2 * slots * side * side,
            transcendentals=0,
        ),
    )(*index, *panels, tiles)


def on_device(seed_class, seed_weight, tile_values, tile_rows, tile_cols, tile_count):
    tiles = tile_values[0, 0]
    rows = tile_rows[0, 0]
    cols = tile_cols[0, 0]
    count = tile_count[0]
    slots, side = tiles.shape[0], tiles.shape[1]
    n_mem, n_clu = lax.axis_size("mem"), lax.axis_size("clu")
    row_blocks, col_blocks = NB_DEV * n_mem, NB_DEV * n_clu
    height = NB_DEV * CLASSES
    row_space, col_space = (row_blocks, CLASSES, side), (col_blocks, CLASSES, side)
    shape = jax.ShapeDtypeStruct

    used = jnp.arange(slots, dtype=jnp.int32) < count
    blocks = jnp.arange(col_blocks, dtype=jnp.int32)[:, None]
    col_table = ((cols[None, :] == blocks) & used).astype(F32)
    col_totals = jnp.sum(tiles, axis=1, dtype=F32)
    col_part = jnp.einsum("kt,tj->kj", col_table, col_totals, precision=lax.Precision.HIGHEST)
    row_part = call_on_tiles(
        functools.partial(totals_kernel, 1), (rows, count), (), tiles,
        shape((row_blocks, side), F32), (row_space,), LIMIT,
    )
    from_cols = swap(col_part.reshape(n_clu, NB_DEV, side), "clu")
    row_part, from_cols = lax.optimization_barrier((row_part, from_cols))
    from_rows = swap(row_part.reshape(n_mem, NB_DEV, side), "mem")
    degree = 1.0 + jnp.sum(from_cols, axis=0) + jnp.sum(from_rows, axis=0)
    inverse_root = lax.rsqrt(degree)

    kinds = seed_class.reshape(NB_DEV, side)
    weight = seed_weight.reshape(NB_DEV, side)
    own = jnp.concatenate([(inverse_root * weight).astype(BF16), kinds.astype(BF16)])
    peers = max(n_mem, n_clu)
    col_own, row_own = gather_both(jnp.broadcast_to(own[None], (peers,) + own.shape))
    kinds, weight, row_own = lax.optimization_barrier((kinds, weight, row_own))
    classes_now = jnp.arange(CLASSES, dtype=jnp.int32)[:, None]

    def panel_of(gathered):
        value = gathered[:, :NB_DEV].reshape(-1, 1, side)
        kind = gathered[:, NB_DEV:].reshape(-1, 1, side)
        return jnp.where(kind == classes_now.astype(BF16), value, jnp.zeros((), BF16))

    labels = jnp.where(kinds[:, None] == classes_now, weight[:, None], jnp.float32(0.0))
    scale = inverse_root[:, None]

    def forward(col_panel):
        return call_on_tiles(
            functools.partial(products_kernel, 1), (rows, count, cols), (col_panel,), tiles,
            shape((n_mem, height, side), BF16), (row_space, col_space), LIMIT,
        )

    def backward(row_panel, dtype):
        return call_on_tiles(
            functools.partial(products_kernel, 0), (cols, count, rows), (row_panel,), tiles,
            shape((n_clu, height, side), dtype), (col_space, row_space), LIMIT,
        )

    def total(parts):
        return jnp.sum(parts.astype(F32), axis=0)

    row_sum = forward(panel_of(col_own).reshape(n_clu, height, side))
    row_sum, row_own = lax.optimization_barrier((row_sum, row_own))
    from_rows = swap(row_sum, "mem")
    col_sum = backward(panel_of(row_own).reshape(n_mem, height, side), F32)
    col_sum, from_rows = lax.optimization_barrier((col_sum, from_rows))
    from_cols = swap(col_sum, "clu")
    first, sent = pl.pallas_call(
        middle_kernel,
        out_shape=(shape((height, side), F32), shape((peers, height, side), BF16)),
        compiler_params=pltpu.CompilerParams(vmem_limit_bytes=LIMIT << 20),
    )(from_cols, from_rows, jnp.broadcast_to(scale, (NB_DEV, CLASSES, side)).reshape(height, side))
    first = first.reshape(NB_DEV, CLASSES, side)

    col_scaled, row_scaled = gather_both(sent)

    def wide(partials):
        return jnp.pad(partials.reshape(-1, NB_DEV, CLASSES * side), ((0, 0), (0, 0), (0, side)))

    row_sum = forward(col_scaled)
    row_wide = wide(row_sum)
    row_sum, row_wide, row_scaled = lax.optimization_barrier((row_sum, row_wide, row_scaled))
    dots = total(row_sum.astype(F32) * row_scaled.astype(F32)).reshape(NB_DEV, CLASSES, side)
    moments = jnp.concatenate(
        [
            jnp.sum(labels * labels, axis=(0, 2)),
            jnp.sum(labels * first, axis=(0, 2)),
            jnp.sum(first * first, axis=(0, 2)),
            2.0 * jnp.sum(dots, axis=(0, 2)),
        ]
    )
    def with_moments(partials, moments):
        pieces = split3(moments)
        pieces = jnp.pad(pieces[None], ((0, NB_DEV - 1), (0, side - pieces.shape[0])))
        pieces = jnp.broadcast_to(pieces[None], (partials.shape[0],) + pieces.shape)
        return lax.dynamic_update_slice(partials, pieces, (0, 0, CLASSES * side))

    def moments_of(swapped):
        pieces = jnp.sum(swapped[:, 0, CLASSES * side :].astype(F32), axis=0)
        return jnp.sum(pieces[: 3 * 4 * CLASSES].reshape(3, -1), axis=0)

    from_rows = swap(with_moments(row_wide, moments), "mem")
    col_wide = wide(backward(row_scaled, BF16))
    col_wide, from_rows = lax.optimization_barrier((col_wide, from_rows))
    from_cols = swap(with_moments(col_wide, moments_of(from_rows)), "clu")
    image = total(from_cols) + total(from_rows)
    second = scale * image[:, : CLASSES * side].reshape(NB_DEV, CLASSES, side)
    m0, m1, m2, m3 = moments_of(from_cols).reshape(4, CLASSES)[:, :, None]

    ratio = m1 / m0
    qq = m2 - ratio * m1
    q_image = m3 - ratio * (2.0 * qq + ratio * m1)
    alpha0 = m0 / (m0 - DAMP * m1)
    pace = DAMP * alpha0
    beta = pace * pace * qq / m0
    alpha1 = qq / (qq - DAMP * q_image - DAMP * pace * qq * (qq / m0))
    q = first - ratio * labels
    q_applied = q - DAMP * (second - ratio * first)
    direction = pace * q + beta * labels
    applied = pace * q_applied + beta * (labels - DAMP * first)
    scores = alpha0 * labels + alpha1 * direction
    residual = pace * q - alpha1 * applied

    def out(x):
        return jnp.swapaxes(x, 0, 1).reshape(CLASSES, NB_DEV * side)

    return (out(scores), out(residual))


def solution(mesh):
    in_specs = (
        P(("clu", "mem")),
        P(("clu", "mem")),
        P("clu", "mem", None, None, None),
        P("clu", "mem", None),
        P("clu", "mem", None),
        P("clu", "mem"),
    )
    out_specs = (P(None, ("clu", "mem")), P(None, ("clu", "mem")))
    return jax.shard_map(
        on_device, mesh=mesh, in_specs=in_specs, out_specs=out_specs, check_vma=False
    )
```

time: 282 us -> 262 us (0.929)
  blocking collectives: 31.9 us -> 11.2 us
  waiting for transfers between devices: 152 us -> 137 us
  Pallas kernels: 0 us -> 14.5 us
  matrix products: 13.4 us -> 0.21 us
  starting transfers between devices: 64.1 us -> 75.9 us
  other arithmetic: 8.53 us -> 11.7 us
    all_to_all x2 -> x1, blocking collectives: 31.9 us -> 11.2 us  [swap(): return lax.all_to_all(parts, axis, 0, 0, tiled=True)]
    all_to_all x8 -> x9, waiting for transfers between devices: 152 us -> 137 us  [swap(): return lax.all_to_all(parts, axis, 0, 0, tiled=True)]
    pallas_call x0 -> x6, Pallas kernels: none -> 14.5 us  [the longest x5 14.5 us: call_on_tiles(): pl.pallas_call(kernel, grid_spec=pltpu.PrefetchScalarGridSpec(num_scalar_...]
    dot_general x10 -> x1, matrix products: 13.4 us -> 0.21 us  [on_device(): jnp.einsum('kt,tj->kj', col_table, col_totals, precision=lax.Precision.HI...]
    all_to_all x8 -> x9, starting transfers between devices: 64.1 us -> 75.9 us  [swap(): return lax.all_to_all(parts, axis, 0, 0, tiled=True)]
    gather x4 -> x0, local copies, waits for them, and re-layouts: 6.45 us -> none  [the longest x2 3.67 us: products(): jnp.take(row_panel, rows, axis=0)]
    reduce_sum x4 -> x10, other arithmetic: 0.15 us -> 4.06 us  [the longest x1 1.29 us: on_device(): jnp.sum(labels * labels, axis=(0, 2))]
    unnamed x30 -> x26, local copies, waits for them, and re-layouts: 0.08 us -> 3.97 us
  transfers between devices with their start and end apart: 8 -> 9, of which waited for: 8 -> 9; matrix products, arithmetic and copies ran while one was open for 4% -> 3% of each run, Pallas kernels for 0% -> 6%
where the time goes in v2:
time: 262 us; the launch traced here: 261 us
  waiting for transfers between devices  137 us (52%)
  starting transfers between devices  75.9 us (29%)
  Pallas kernels  14.5 us (6%)
  other arithmetic  11.7 us (4%)
  blocking collectives  11.2 us (4%)
  local copies, waits for them, and re-layouts  9.48 us (4%)
    all_to_all x9, waiting for transfers between devices, swap(): return lax.all_to_all(parts, axis, 0, 0, tiled=True)  137 us
    all_to_all x9, starting transfers between devices, swap(): return lax.all_to_all(parts, axis, 0, 0, tiled=True)  75.9 us
    pallas_call x5, Pallas kernels, call_on_tiles(): pl.pallas_call(kernel, grid_spec=pltpu.PrefetchScalarGridSpec(num_scalar_...  14.5 us
    all_to_all x1, blocking collectives, swap(): return lax.all_to_all(parts, axis, 0, 0, tiled=True)  11.2 us
  transfers between devices with their start and end apart: 9, of which 9 were waited for; matrix products, arithmetic and copies ran while one was open for 3% of the time, Pallas kernels for 6%

profile of v2, /device:TPU:1, one launch (start us, length us, event | category | flops | bytes accessed | tf_op | source)
XLA Modules:
  0.0 261.4 jit_solution(13555973071875742891)
XLA Ops:
  1.5 2.9 %convert_reduce_fusion = f32[96,128]{1,0:T(8,128)S(1)} fusion(bf16[1,1,96,128,128]{4,3,2,1,0:T(8,128)(2,1)} %param.8), kind=kLoop, calls=%fused_computation | loop fusion | flops 3133440 | bytes 3194880 | tf_op jit(solution)/shard_map/reduce_sum | solution.py:129
  4.4 0.2 fusion
  4.6 0.6 copy.8
  5.3 17.6 %all-to-all-start = ((f32[32,2,128]{2,1,0:T(2,128)}), f32[32,2,128]{2,1,0:T(2,128)S(1)}, u32[]{:S(2)}, u32[]{:S(2)}) async-start(f32[32,2,128]{2,1,0:T(2,128)} %copy.8), calls=%async_computation | async-start | bytes 65536 | tf_op jit(solution)/shard_map/all_to_all | solution.py:20
  22.9 3.5 %shard_map.77 = f32[64,128]{1,0:T(8,128)} custom-call(s32[96]{0:T(128)S(1)} %bitcast.105, s32[1]{0:T(128)} %bitcast.94.count_ref, bf16[96,128,128]{2,1,0:T(8,128)(2,1)S(1)} %bitcast.100), custom_call_target="tpu_custom_call" | custom-call | flops 25165824 | bytes 3145728 | tf_op jit(solution)/shard_map/pallas_call | solution.py:92
  26.5 3.8 %all-to-all-done = f32[32,2,128]{2,1,0:T(2,128)S(1)} async-done(((f32[32,2,128]{2,1,0:T(2,128)}), f32[32,2,128]{2,1,0:T(2,128)S(1)}, u32[]{:S(2)}, u32[]{:S(2)}) %all-to-all-start) | async-done | bytes 32800 | tf_op jit(solution)/shard_map/all_to_all | solution.py:20
  30.3 19.3 %all-to-all-start.1 = ((f32[32,2,128]{2,1,0:T(2,128)}), f32[32,2,128]{2,1,0:T(2,128)S(1)}, u32[]{:S(2)}, u32[]{:S(2)}) async-start(f32[32,2,128]{2,1,0:T(2,128)} %bitcast.6), calls=%async_computation.1 | async-start | bytes 65536 | tf_op jit(solution)/shard_map/all_to_all | solution.py:20
  49.7 21.9 %all-to-all-done.1 = f32[32,2,128]{2,1,0:T(2,128)S(1)} async-done(((f32[32,2,128]{2,1,0:T(2,128)}), f32[32,2,128]{2,1,0:T(2,128)S(1)}, u32[]{:S(2)}, u32[]{:S(2)}) %all-to-all-start.1) | async-done | bytes 32800 | tf_op jit(solution)/shard_map/all_to_all | solution.py:20
  71.6 0.6 multiply_convert_fusion
  72.2 0.6 broadcast_in_dim.50
  72.8 5.6 %all-to-all-start.2 = ((bf16[32,4,128]{2,1,0:T(4,128)(2,1)}), bf16[32,4,128]{2,1,0:T(4,128)(2,1)S(1)}, u32[]{:S(2)}, u32[]{:S(2)}) async-start(bf16[32,4,128]{2,1,0:T(4,128)(2,1)} %broadcast_in_dim.50), calls=%async_computation.2 | async-start | bytes 65536 | tf_op jit(solution)/shard_map/all_to_all | solution.py:20
  78.5 0.1 eq.98
  78.6 7.3 %all-to-all-done.2 = bf16[32,4,128]{2,1,0:T(4,128)(2,1)S(1)} async-done(((bf16[32,4,128]{2,1,0:T(4,128)(2,1)}), bf16[32,4,128]{2,1,0:T(4,128)(2,1)S(1)}, u32[]{:S(2)}, u32[]{:S(2)}) %all-to-all-start.2) | async-done | bytes 32800 | tf_op jit(solution)/shard_map/all_to_all | solution.py:20
  85.8 3.9 %all-to-all-start.3 = ((bf16[32,4,128]{2,1,0:T(4,128)(2,1)}), bf16[32,4,128]{2,1,0:T(4,128)(2,1)S(1)}, u32[]{:S(2)}, u32[]{:S(2)}) async-start(bf16[32,4,128]{2,1,0:T(4,128)(2,1)} %broadcast_in_dim.50), calls=%async_computation.3 | async-start | bytes 65536 | tf_op jit(solution)/shard_map/all_to_all | solution.py:20
  89.8 0.1 compare_select_fusion.1.panel
  89.9 3.6 %shard_map.78 = bf16[32,16,128]{2,1,0:T(8,128)(2,1)} custom-call(s32[96]{0:T(128)S(1)} %bitcast.106, s32[1]{0:T(128)} %bitcast.95.count_ref, s32[96]{0:T(128)S(1)} %bitcast.111, bf16[32,16,128]{2,1,0:T(8,128)(2,1)S(1)} %compare_select_fusion.1.panel, bf16[96,128,128]{2,1,0:T(8,128)(2,1)S(1)} %bitcast.101), custom_call_target="tpu_custom_call" | custom-call | flops 25165824 | bytes 3145728 | tf_op jit(solution)/shard_map/pallas_call | solution.py:92
  93.5 18.3 %all-to-all-done.3 = bf16[32,4,128]{2,1,0:T(4,128)(2,1)S(1)} async-done(((bf16[32,4,128]{2,1,0:T(4,128)(2,1)}), bf16[32,4,128]{2,1,0:T(4,128)(2,1)S(1)}, u32[]{:S(2)}, u32[]{:S(2)}) %all-to-all-start.3) | async-done | bytes 32800 | tf_op jit(solution)/shard_map/all_to_all | solution.py:20
  111.8 3.8 %all-to-all-start.4 = ((bf16[32,16,128]{2,1,0:T(8,128)(2,1)}), bf16[32,16,128]{2,1,0:T(8,128)(2,1)S(1)}, u32[]{:S(2)}, u32[]{:S(2)}) async-start(bf16[32,16,128]{2,1,0:T(8,128)(2,1)} %shard_map.78), calls=%async_computation.4 | async-start | bytes 262144 | tf_op jit(solution)/shard_map/all_to_all | solution.py:20
  115.7 0.1 compare_select_fusion.panel
  115.8 2.2 shard_map.79
  118.0 0.7 copy-done.1
  118.7 24.8 %all-to-all-done.4.from_rows = bf16[32,16,128]{2,1,0:T(8,128)(2,1)S(1)} async-done(((bf16[32,16,128]{2,1,0:T(8,128)(2,1)}), bf16[32,16,128]{2,1,0:T(8,128)(2,1)S(1)}, u32[]{:S(2)}, u32[]{:S(2)}) %all-to-all-start.4) | async-done | bytes 131104 | tf_op jit(solution)/shard_map/all_to_all | solution.py:20
  143.4 8.2 %all-to-all-start.5 = ((f32[32,16,128]{2,1,0:T(8,128)}), f32[32,16,128]{2,1,0:T(8,128)S(1)}, u32[]{:S(2)}, u32[]{:S(2)}) async-start(f32[32,16,128]{2,1,0:T(8,128)} %copy-done.1), calls=%async_computation.5 | async-start | bytes 524288 | tf_op jit(solution)/shard_map/all_to_all | solution.py:20
  151.7 0.7 broadcast_bitcast_fusion.scale
  152.3 8.3 %all-to-all-done.5.from_cols = f32[32,16,128]{2,1,0:T(8,128)S(1)} async-done(((f32[32,16,128]{2,1,0:T(8,128)}), f32[32,16,128]{2,1,0:T(8,128)S(1)}, u32[]{:S(2)}, u32[]{:S(2)}) %all-to-all-start.5) | async-done | bytes 262176 | tf_op jit(solution)/shard_map/all_to_all | solution.py:20
  160.7 0.1 shard_map.80
  160.7 0.6 copy-done.2
  161.4 11.2 %all_to_all.50.panel = bf16[32,16,128]{2,1,0:T(8,128)(2,1)S(1)} all-to-all(bf16[32,16,128]{2,1,0:T(8,128)(2,1)S(1)} %get-tuple-element.33), channel_id=1, replica_groups=mesh['clu'=32,'mem'=32] {'clu'}, dimensions={0} | all-to-all | bytes 262144 | tf_op jit(solution)/shard_map/all_to_all | solution.py:20
  172.5 3.9 %all-to-all-start.7 = ((bf16[32,16,128]{2,1,0:T(8,128)(2,1)}), bf16[32,16,128]{2,1,0:T(8,128)(2,1)S(1)}, u32[]{:S(2)}, u32[]{:S(2)}) async-start(bf16[32,16,128]{2,1,0:T(8,128)(2,1)} %copy-done.2), calls=%async_computation.7 | async-start | bytes 262144 | tf_op jit(solution)/shard_map/all_to_all | solution.py:20
  176.4 0.1 eq.110
  176.5 1.3 fusion.8
  177.8 0.9 fusion.25
  178.7 0.1 reduce_sum.147
  178.8 0.5 reduce_sum.148
  179.3 0.1 reduce_sum.150
  179.4 0.5 reduce_sum.151
  179.9 0.7 copy-done.4
  180.6 0.7 copy-done.7
  181.2 3.0 %shard_map.81 = bf16[32,16,128]{2,1,0:T(8,128)(2,1)S(1)} custom-call(s32[96]{0:T(128)S(1)} %bitcast.108, s32[1]{0:T(128)} %bitcast.97.count_ref, s32[96]{0:T(128)S(1)} %bitcast.113, bf16[32,16,128]{2,1,0:T(8,128)(2,1)S(1)} %all_to_all.50.panel, bf16[96,128,128]{2,1,0:T(8,128)(2,1)S(1)} %bitcast.103), custom_call_target="tpu_custom_call" | custom-call | flops 25165824 | bytes 3145728 | tf_op jit(solution)/shard_map/pallas_call | solution.py:92
  184.2 0.8 pad.14
  185.0 21.5 %all-to-all-done.7.panel = bf16[32,16,128]{2,1,0:T(8,128)(2,1)S(1)} async-done(((bf16[32,16,128]{2,1,0:T(8,128)(2,1)}), bf16[32,16,128]{2,1,0:T(8,128)(2,1)S(1)}, u32[]{:S(2)}, u32[]{:S(2)}) %all-to-all-start.7) | async-done | bytes 131104 | tf_op jit(solution)/shard_map/all_to_all | solution.py:20
  206.5 0.2 multiply_reduce_fusion
  206.7 0.1 reduce_sum.153
  206.8 0.7 fusion.33
  207.5 0.1 fusion.45
  207.6 0.6 broadcast_dynamic-update-slice_fusion.1
  208.3 4.6 %all-to-all-start.8 = ((bf16[32,2,1152]{2,1,0:T(2,128)(2,1)}), bf16[32,2,1152]{2,1,0:T(2,128)(2,1)}, u32[]{:S(2)}, u32[]{:S(2)}) async-start(bf16[32,2,1152]{2,1,0:T(2,128)(2,1)} %broadcast_dynamic-update-slice_fusion.1), calls=%async_computation.8 | async-start | bytes 294912 | tf_op jit(solution)/shard_map/all_to_all | solution.py:20
  212.8 0.6 copy-done.5
  213.5 0.7 copy-done.8
  214.1 2.2 shard_map.82
  216.4 0.8 pad.15
  217.1 23.9 %all-to-all-done.8 = bf16[32,2,1152]{2,1,0:T(2,128)(2,1)} async-done(((bf16[32,2,1152]{2,1,0:T(2,128)(2,1)}), bf16[32,2,1152]{2,1,0:T(2,128)(2,1)}, u32[]{:S(2)}, u32[]{:S(2)}) %all-to-all-start.8) | async-done | bytes 147488 | tf_op jit(solution)/shard_map/all_to_all | solution.py:20
  241.0 0.8 convert_reduce_fusion.3
  241.8 0.1 reshape.345
  241.9 0.1 fusion.50
  242.0 0.6 broadcast_dynamic-update-slice_fusion
  242.6 9.0 %all-to-all-start.9 = ((bf16[32,2,1152]{2,1,0:T(2,128)(2,1)}), bf16[32,2,1152]{2,1,0:T(2,128)(2,1)S(1)}, u32[]{:S(2)}, u32[]{:S(2)}) async-start(bf16[32,2,1152]{2,1,0:T(2,128)(2,1)} %broadcast_dynamic-update-slice_fusion), calls=%async_computation.9 | async-start | bytes 294912 | tf_op jit(solution)/shard_map/all_to_all | solution.py:20
  251.6 1.0 convert_reduce_fusion.1
  252.7 6.8 %all-to-all-done.9 = bf16[32,2,1152]{2,1,0:T(2,128)(2,1)S(1)} async-done(((bf16[32,2,1152]{2,1,0:T(2,128)(2,1)}), bf16[32,2,1152]{2,1,0:T(2,128)(2,1)S(1)}, u32[]{:S(2)}, u32[]{:S(2)}) %all-to-all-start.9) | async-done | bytes 147488 | tf_op jit(solution)/shard_map/all_to_all | solution.py:20
  259.6 0.1 reshape.346
  259.7 0.1 subtract_divide_fusion.1
  259.8 0.1 broadcast_multiply_fusion
  259.9 0.1 convert_reduce_fusion.2
  260.0 1.3 fusion.18
  (45 shorter events, 0.5 us)
Async XLA Ops:
  0.6 22.3 %copy-start = (bf16[1,1,96,128,128]{4,3,2,1,0:T(8,128)(2,1)S(1)}, bf16[1,1,96,128,128]{4,3,2,1,0:T(8,128)(2,1)}, u32[]{:S(2)}) copy-start(bf16[1,1,96,128,128]{4,3,2,1,0:T(8,128)(2,1)} %param.8) | copy-start | bytes 9437188
  0.6 3.8 %copy-start.6 = (s32[1,1,96]{2,1,0:T(1,128)S(1)}, s32[1,1,96]{2,1,0:T(1,128)}, u32[]{:S(2)}) copy-start(s32[1,1,96]{2,1,0:T(1,128)} %param.10) | copy-start | bytes 1156
  0.7 22.3 %copy-start.3 = (s32[1,1,96]{2,1,0:T(1,128)S(1)}, s32[1,1,96]{2,1,0:T(1,128)}, u32[]{:S(2)}) copy-start(s32[1,1,96]{2,1,0:T(1,128)} %param.9) | copy-start | bytes 1156
  1.5 48.1 %copy-start.11 = (s32[256]{0:T(256)S(1)}, s32[256]{0:T(256)}, u32[]{:S(2)}) copy-start(s32[256]{0:T(256)} %param.6) | copy-start | bytes 3076
  1.5 70.1 %copy-start.9 = (f32[256]{0:T(256)S(1)}, f32[256]{0:T(256)}, u32[]{:S(2)}) copy-start(f32[256]{0:T(256)} %param.7) | copy-start | bytes 3076
  5.3 25.0 %all-to-all-start = ((f32[32,2,128]{2,1,0:T(2,128)}), f32[32,2,128]{2,1,0:T(2,128)S(1)}, u32[]{:S(2)}, u32[]{:S(2)}) async-start(f32[32,2,128]{2,1,0:T(2,128)} %copy.8), calls=%async_computation | async-start | bytes 65536 | tf_op jit(solution)/shard_map/all_to_all | solution.py:20
  30.3 41.3 %all-to-all-start.1 = ((f32[32,2,128]{2,1,0:T(2,128)}), f32[32,2,128]{2,1,0:T(2,128)S(1)}, u32[]{:S(2)}, u32[]{:S(2)}) async-start(f32[32,2,128]{2,1,0:T(2,128)} %bitcast.6), calls=%async_computation.1 | async-start | bytes 65536 | tf_op jit(solution)/shard_map/all_to_all | solution.py:20
  72.8 13.0 %all-to-all-start.2 = ((bf16[32,4,128]{2,1,0:T(4,128)(2,1)}), bf16[32,4,128]{2,1,0:T(4,128)(2,1)S(1)}, u32[]{:S(2)}, u32[]{:S(2)}) async-start(bf16[32,4,128]{2,1,0:T(4,128)(2,1)} %broadcast_in_dim.50), calls=%async_computation.2 | async-start | bytes 65536 | tf_op jit(solution)/shard_map/all_to_all | solution.py:20
  85.8 26.0 %all-to-all-start.3 = ((bf16[32,4,128]{2,1,0:T(4,128)(2,1)}), bf16[32,4,128]{2,1,0:T(4,128)(2,1)S(1)}, u32[]{:S(2)}, u32[]{:S(2)}) async-start(bf16[32,4,128]{2,1,0:T(4,128)(2,1)} %broadcast_in_dim.50), calls=%async_computation.3 | async-start | bytes 65536 | tf_op jit(solution)/shard_map/all_to_all | solution.py:20
  111.8 31.7 %all-to-all-start.4 = ((bf16[32,16,128]{2,1,0:T(8,128)(2,1)}), bf16[32,16,128]{2,1,0:T(8,128)(2,1)S(1)}, u32[]{:S(2)}, u32[]{:S(2)}) async-start(bf16[32,16,128]{2,1,0:T(8,128)(2,1)} %shard_map.78), calls=%async_computation.4 | async-start | bytes 262144 | tf_op jit(solution)/shard_map/all_to_all | solution.py:20
  118.0 0.7 copy-start.1
  143.4 17.2 %all-to-all-start.5 = ((f32[32,16,128]{2,1,0:T(8,128)}), f32[32,16,128]{2,1,0:T(8,128)S(1)}, u32[]{:S(2)}, u32[]{:S(2)}) async-start(f32[32,16,128]{2,1,0:T(8,128)} %copy-done.1), calls=%async_computation.5 | async-start | bytes 524288 | tf_op jit(solution)/shard_map/all_to_all | solution.py:20
  160.7 0.6 copy-start.2
  172.5 34.0 %all-to-all-start.7 = ((bf16[32,16,128]{2,1,0:T(8,128)(2,1)}), bf16[32,16,128]{2,1,0:T(8,128)(2,1)S(1)}, u32[]{:S(2)}, u32[]{:S(2)}) async-start(bf16[32,16,128]{2,1,0:T(8,128)(2,1)} %copy-done.2), calls=%async_computation.7 | async-start | bytes 262144 | tf_op jit(solution)/shard_map/all_to_all | solution.py:20
  179.9 0.7 copy-start.4
  180.6 0.7 copy-start.7
  184.2 75.8 %copy-start.10 = (f32[256]{0:T(256)S(1)}, f32[256]{0:T(256)}, u32[]{:S(2)}) copy-start(f32[256]{0:T(256)} %param.7) | copy-start | bytes 3076
  184.2 75.8 %copy-start.12 = (s32[256]{0:T(256)S(1)}, s32[256]{0:T(256)}, u32[]{:S(2)}) copy-start(s32[256]{0:T(256)} %param.6) | copy-start | bytes 3076
  208.3 32.7 %all-to-all-start.8 = ((bf16[32,2,1152]{2,1,0:T(2,128)(2,1)}), bf16[32,2,1152]{2,1,0:T(2,128)(2,1)}, u32[]{:S(2)}, u32[]{:S(2)}) async-start(bf16[32,2,1152]{2,1,0:T(2,128)(2,1)} %broadcast_dynamic-update-slice_fusion.1), calls=%async_computation.8 | async-start | bytes 294912 | tf_op jit(solution)/shard_map/all_to_all | solution.py:20
  212.8 0.7 copy-start.5
  213.5 0.7 copy-start.8
  242.6 16.9 %all-to-all-start.9 = ((bf16[32,2,1152]{2,1,0:T(2,128)(2,1)}), bf16[32,2,1152]{2,1,0:T(2,128)(2,1)S(1)}, u32[]{:S(2)}, u32[]{:S(2)}) async-start(bf16[32,2,1152]{2,1,0:T(2,128)(2,1)} %broadcast_dynamic-update-slice_fusion), calls=%async_computation.9 | async-start | bytes 294912 | tf_op jit(solution)/shard_map/all_to_all | solution.py:20

commit v3 on v2

v3 whole, which is shorter than its diff:
```python
import functools

import jax
import jax.numpy as jnp
from jax import lax
from jax.experimental import pallas as pl
from jax.experimental.pallas import tpu as pltpu
from jax.sharding import PartitionSpec as P

CLASSES = 8
NB_DEV = 2
DAMP = 0.99
F32 = jnp.float32
BF16 = jnp.bfloat16
STEP = 32
LIMIT = 8


def swap(parts, axis):
    return lax.all_to_all(parts, axis, 0, 0, tiled=True)


def split3(x):
    high = lax.reduce_precision(x, 8, 7)
    rest = x - high
    mid = lax.reduce_precision(rest, 8, 7)
    return jnp.concatenate([high, mid, rest - mid]).astype(BF16)


def sum_slots(into_ref, count_ref, tiles_ref, acc, left_of, side):
    acc[...] = jnp.zeros_like(acc)
    for slot in range(tiles_ref.shape[0]):
        used = jnp.where(slot < count_ref[0], 1.0, 0.0)
        product = lax.dot_general(
            left_of(slot), tiles_ref[slot], (((1,), (side,)), ((), ())), preferred_element_type=F32
        )
        acc[into_ref[slot]] += used * product


def totals_kernel(side, into_ref, count_ref, tiles_ref, out, acc):
    ones = jnp.ones((CLASSES, tiles_ref.shape[2]), BF16)
    sum_slots(into_ref, count_ref, tiles_ref, acc, lambda slot: ones, side)
    out[...] = acc[:, 0, :]


def products_kernel(side, into_ref, count_ref, from_ref, panel, tiles_ref, out, acc, wide):
    wide[...] = panel[...].astype(F32).reshape(wide.shape)
    sum_slots(
        into_ref, count_ref, tiles_ref, acc, lambda slot: wide[from_ref[slot]].astype(BF16), side
    )
    out[...] = acc[...].reshape(out.shape).astype(out.dtype)


def middle_kernel(from_cols, row_image, scale, first, sent):
    scale = scale[...]
    image = scale * (jnp.sum(from_cols[...], axis=0) + row_image[...])
    first[...] = image
    sent[...] = jnp.broadcast_to((scale * image).astype(BF16)[None], sent.shape)


def call_on_tiles(kernel, index, panels, tiles, out, scratch, limit):
    slots, side = tiles.shape[0], tiles.shape[1]

    smem, vmem = pl.BlockSpec(memory_space=pltpu.SMEM), pl.BlockSpec(memory_space=pltpu.VMEM)
    return pl.pallas_call(
        kernel,
        in_specs=[smem] * len(index) + [vmem] * (len(panels) + 1),
        out_specs=vmem,
        scratch_shapes=[pltpu.VMEM(x, F32) for x in scratch],
        out_shape=out,
        compiler_params=pltpu.CompilerParams(vmem_limit_bytes=limit << 20),
        cost_estimate=pl.CostEstimate(
            flops=2 * CLASSES * slots * side * side,
            bytes_accessed=2 * slots * side * side,
            transcendentals=0,
        ),
    )(*index, *panels, tiles)


def on_device(seed_class, seed_weight, tile_values, tile_rows, tile_cols, tile_count):
    tiles = tile_values[0, 0]
    rows = tile_rows[0, 0]
    cols = tile_cols[0, 0]
    count = tile_count[0]
    slots, side = tiles.shape[0], tiles.shape[1]
    n_mem, n_clu = lax.axis_size("mem"), lax.axis_size("clu")
    row_blocks, col_blocks = NB_DEV * n_mem, NB_DEV * n_clu
    height = NB_DEV * CLASSES
    row_space, col_space = (row_blocks, CLASSES, side), (col_blocks, CLASSES, side)
    shape = jax.ShapeDtypeStruct

    used = jnp.arange(slots, dtype=jnp.int32) < count
    blocks = jnp.arange(col_blocks, dtype=jnp.int32)[:, None]
    col_table = ((cols[None, :] == blocks) & used).astype(F32)
    col_totals = jnp.sum(tiles, axis=1, dtype=F32)
    col_part = jnp.einsum("kt,tj->kj", col_table, col_totals, precision=lax.Precision.HIGHEST)
    row_part = call_on_tiles(
        functools.partial(totals_kernel, 1), (rows, count), (), tiles,
        shape((row_blocks, side), F32), (row_space,), LIMIT,
    )
    from_cols = swap(col_part.reshape(n_clu, NB_DEV, side), "clu")
    row_part, from_cols = lax.optimization_barrier((row_part, from_cols))
    from_rows = swap(row_part.reshape(n_mem, NB_DEV, side), "mem")
    degree = 1.0 + jnp.sum(from_cols, axis=0) + jnp.sum(from_rows, axis=0)
    inverse_root = lax.rsqrt(degree)

    kinds = seed_class.reshape(NB_DEV, side)
    weight = seed_weight.reshape(NB_DEV, side)
    own = jnp.concatenate([inverse_root * weight, kinds.astype(F32)])
    peers = max(n_mem, n_clu)
    col_own = swap(jnp.broadcast_to(own.astype(BF16)[None], (n_clu,) + own.shape), "clu")
    classes_now = jnp.arange(CLASSES, dtype=jnp.int32)[:, None]

    def panel_of(value, kind):
        kind = kind.reshape(-1, 1, side)
        panel = jnp.where(kind == classes_now.astype(BF16), value.reshape(-1, 1, side), jnp.zeros((), BF16))
        return panel.reshape(-1, height, side)

    labels = jnp.where(kinds[:, None] == classes_now, weight[:, None], jnp.float32(0.0))
    scale = inverse_root[:, None]

    def forward(col_panel):
        return call_on_tiles(
            functools.partial(products_kernel, 1), (rows, count, cols), (col_panel,), tiles,
            shape((n_mem, height, side), BF16), (row_space, col_space), LIMIT,
        )

    def backward(row_panel, dtype):
        return call_on_tiles(
            functools.partial(products_kernel, 0), (cols, count, rows), (row_panel,), tiles,
            shape((n_clu, height, side), dtype), (col_space, row_space), LIMIT,
        )

    def total(parts):
        return jnp.sum(parts.astype(F32), axis=0)

    lanes = CLASSES * side

    def wide(partials, tail):
        partials = partials.reshape(-1, NB_DEV, lanes)
        tail = jnp.broadcast_to(tail[None].astype(BF16), partials.shape[:1] + tail.shape)
        return jnp.concatenate([partials, tail], axis=2)

    def narrow(image):
        return image[:, :lanes].reshape(NB_DEV, CLASSES, side)

    row_sum = forward(panel_of(col_own[:, :NB_DEV], col_own[:, NB_DEV:]))
    from_mem = swap(wide(row_sum, jnp.concatenate([own[:NB_DEV], own[NB_DEV:]], axis=1)), "mem")
    col_sum = backward(
        panel_of(from_mem[:, :, lanes : lanes + side], from_mem[:, :, lanes + side :]), F32
    )
    from_cols = swap(col_sum, "clu")
    row_image = narrow(total(from_mem)).reshape(height, side)
    first, sent = pl.pallas_call(
        middle_kernel,
        out_shape=(shape((height, side), F32), shape((peers, height, side), BF16)),
        compiler_params=pltpu.CompilerParams(vmem_limit_bytes=LIMIT << 20),
    )(from_cols, row_image, jnp.broadcast_to(scale, (NB_DEV, CLASSES, side)).reshape(height, side))
    first = first.reshape(NB_DEV, CLASSES, side)

    col_scaled = swap(sent[:n_clu], "clu")
    sent, col_scaled = lax.optimization_barrier((sent, col_scaled))
    row_scaled = swap(sent[:n_mem], "mem")
    def pieces_row(x):
        pieces = split3(x)
        return jnp.pad(pieces, (0, side - pieces.shape[0]))

    def whole(pieces, count):
        return jnp.sum(pieces[: 3 * count].reshape(3, count), axis=0)

    early = jnp.concatenate(
        [
            jnp.sum(labels * labels, axis=(0, 2)),
            jnp.sum(labels * first, axis=(0, 2)),
            jnp.sum(first * first, axis=(0, 2)),
        ]
    )
    row_sum = forward(col_scaled)
    row_wide = wide(row_sum, jnp.pad(pieces_row(early)[None], ((0, NB_DEV - 1), (0, 0))))
    row_sum, row_wide, row_scaled = lax.optimization_barrier((row_sum, row_wide, row_scaled))
    dots = 2.0 * jnp.sum(
        (row_sum.astype(F32) * row_scaled.astype(F32)).reshape(-1, NB_DEV, CLASSES, side), axis=(0, 1, 3)
    )
    is_late = jnp.arange(NB_DEV)[:, None] == 1
    spare = jnp.where(is_late, pieces_row(dots), row_wide[:, :, lanes:])
    from_rows = swap(lax.dynamic_update_slice(row_wide, spare, (0, 0, lanes)), "mem")
    col_sum = backward(row_scaled, BF16)
    col_sum, from_rows = lax.optimization_barrier((col_sum, from_rows))
    from_rows = lax.optimization_barrier(total(from_rows))
    line = from_rows[:, lanes:]
    line = pieces_row(jnp.concatenate([whole(line[0], 3 * CLASSES), whole(line[1], CLASSES)]))
    line = jnp.broadcast_to(jnp.pad(line[None], ((0, CLASSES - 1), (0, 0))), (n_clu, CLASSES, side))
    from_cols = swap(jnp.concatenate([col_sum, line], axis=1), "clu")
    from_cols, row_image = lax.optimization_barrier((from_cols, narrow(from_rows)))
    from_cols = total(from_cols)
    image = from_cols[:height].reshape(NB_DEV, CLASSES, side) + row_image
    second = scale * image
    m0, m1, m2, m3 = whole(from_cols[height], 4 * CLASSES).reshape(4, CLASSES)[:, :, None]

    ratio = m1 / m0
    qq = m2 - ratio * m1
    q_image = m3 - ratio * (2.0 * qq + ratio * m1)
    alpha0 = m0 / (m0 - DAMP * m1)
    pace = DAMP * alpha0
    beta = pace * pace * qq / m0
    alpha1 = qq / (qq - DAMP * q_image - DAMP * pace * qq * (qq / m0))
    q = first - ratio * labels
    q_applied = q - DAMP * (second - ratio * first)
    direction = pace * q + beta * labels
    applied = pace * q_applied + beta * (labels - DAMP * first)
    scores = alpha0 * labels + alpha1 * direction
    residual = pace * q - alpha1 * applied

    def out(x):
        return jnp.swapaxes(x, 0, 1).reshape(CLASSES, NB_DEV * side)

    return (out(scores), out(residual))


def solution(mesh):
    in_specs = (
        P(("clu", "mem")),
        P(("clu", "mem")),
        P("clu", "mem", None, None, None),
        P("clu", "mem", None),
        P("clu", "mem", None),
        P("clu", "mem"),
    )
    out_specs = (P(None, ("clu", "mem")), P(None, ("clu", "mem")))
    return jax.shard_map(
        on_device, mesh=mesh, in_specs=in_specs, out_specs=out_specs, check_vma=False
    )
```

time: 262 us -> 244 us (0.931)
  waiting for transfers between devices: 137 us -> 109 us
  blocking collectives: 11.2 us -> 36 us
  starting transfers between devices: 75.9 us -> 69.5 us
  local copies, waits for them, and re-layouts: 9.48 us -> 4.74 us
  Pallas kernels: 14.5 us -> 11.3 us
    all_to_all x9 -> x8, waiting for transfers between devices: 137 us -> 109 us  [swap(): return lax.all_to_all(parts, axis, 0, 0, tiled=True)]
    all_to_all x1, blocking collectives: 11.2 us -> 36 us  [swap(): return lax.all_to_all(parts, axis, 0, 0, tiled=True)]
    all_to_all x9 -> x8, starting transfers between devices: 75.9 us -> 69.5 us  [swap(): return lax.all_to_all(parts, axis, 0, 0, tiled=True)]
    pallas_call x5, Pallas kernels: 14.5 us -> 10.6 us  [call_on_tiles(): pl.pallas_call(kernel, in_specs=[smem] * len(index) + [vmem] * (len(panel...]
    unnamed x26 -> x18, local copies, waits for them, and re-layouts: 3.97 us -> 1.3 us
  transfers between devices with their start and end apart: 9 -> 8, of which waited for: 9 -> 8; matrix products, arithmetic and copies ran while one was open for 3% -> 2% of each run, Pallas kernels for 6% -> 3%
where the time goes in v3:
time: 244 us
  waiting for transfers between devices  109 us (45%)
  starting transfers between devices  69.5 us (28%)
  blocking collectives  36 us (15%)
  other arithmetic  11.5 us (5%)
  Pallas kernels  11.3 us (5%)
  local copies, waits for them, and re-layouts  4.74 us (2%)
    all_to_all x8, waiting for transfers between devices, swap(): return lax.all_to_all(parts, axis, 0, 0, tiled=True)  109 us
    all_to_all x8, starting transfers between devices, swap(): return lax.all_to_all(parts, axis, 0, 0, tiled=True)  69.5 us
    all_to_all x1, blocking collectives, swap(): return lax.all_to_all(parts, axis, 0, 0, tiled=True)  36 us
    pallas_call x5, Pallas kernels, call_on_tiles(): pl.pallas_call(kernel, in_specs=[smem] * len(index) + [vmem] * (len(panel...  10.6 us
  transfers between devices with their start and end apart: 8, of which 8 were waited for; matrix products, arithmetic and copies ran while one was open for 2% of the time, Pallas kernels for 3%

profile of v3, /device:TPU:1, one launch (start us, length us, event | category | flops | bytes accessed | tf_op | source)
XLA Modules:
  0.0 243.6 jit_solution(17129088531582790889)
XLA Ops:
  0.6 0.0 copy-start
  0.6 0.0 copy-start.2
  0.7 0.0 copy-start.3
  1.5 0.0 copy-start.6
  1.5 0.0 copy-start.5
  1.5 2.9 %convert_reduce_fusion = f32[96,128]{1,0:T(8,128)S(1)} fusion(bf16[1,1,96,128,128]{4,3,2,1,0:T(8,128)(2,1)} %param.8), kind=kLoop, calls=%fused_computation | loop fusion | flops 3133440 | bytes 3194880 | tf_op jit(solution)/shard_map/reduce_sum | solution.py:95
  4.4 0.2 fusion
  4.6 0.6 copy.8
  5.3 17.6 %all-to-all-start = ((f32[32,2,128]{2,1,0:T(2,128)}), f32[32,2,128]{2,1,0:T(2,128)S(1)}, u32[]{:S(2)}, u32[]{:S(2)}) async-start(f32[32,2,128]{2,1,0:T(2,128)} %copy.8), calls=%async_computation | async-start | bytes 65536 | tf_op jit(solution)/shard_map/all_to_all | solution.py:20
  22.9 2.9 %shard_map.77 = f32[64,128]{1,0:T(8,128)} custom-call(s32[96]{0:T(128)S(1)} %bitcast.107, s32[1]{0:T(128)} %bitcast.91.count_ref, bf16[96,128,128]{2,1,0:T(8,128)(2,1)S(1)} %bitcast.97), custom_call_target="tpu_custom_call" | custom-call | flops 25165824 | bytes 3145728 | tf_op jit(solution)/shard_map/pallas_call | solution.py:65
  25.9 4.4 %all-to-all-done = f32[32,2,128]{2,1,0:T(2,128)S(1)} async-done(((f32[32,2,128]{2,1,0:T(2,128)}), f32[32,2,128]{2,1,0:T(2,128)S(1)}, u32[]{:S(2)}, u32[]{:S(2)}) %all-to-all-start) | async-done | bytes 32800 | tf_op jit(solution)/shard_map/all_to_all | solution.py:20
  30.3 19.3 %all-to-all-start.1 = ((f32[32,2,128]{2,1,0:T(2,128)}), f32[32,2,128]{2,1,0:T(2,128)S(1)}, u32[]{:S(2)}, u32[]{:S(2)}) async-start(f32[32,2,128]{2,1,0:T(2,128)} %bitcast.6), calls=%async_computation.1 | async-start | bytes 65536 | tf_op jit(solution)/shard_map/all_to_all | solution.py:20
  49.6 0.1 eq.104
  49.7 21.8 %all-to-all-done.1 = f32[32,2,128]{2,1,0:T(2,128)S(1)} async-done(((f32[32,2,128]{2,1,0:T(2,128)}), f32[32,2,128]{2,1,0:T(2,128)S(1)}, u32[]{:S(2)}, u32[]{:S(2)}) %all-to-all-start.1) | async-done | bytes 32800 | tf_op jit(solution)/shard_map/all_to_all | solution.py:20
  71.7 0.6 broadcast_in_dim.103
  72.3 5.6 %all-to-all-start.2 = ((bf16[32,4,128]{2,1,0:T(4,128)(2,1)}), bf16[32,4,128]{2,1,0:T(4,128)(2,1)S(1)}, u32[]{:S(2)}, u32[]{:S(2)}) async-start(bf16[32,4,128]{2,1,0:T(4,128)(2,1)} %broadcast_in_dim.103), calls=%async_computation.2 | async-start | bytes 65536 | tf_op jit(solution)/shard_map/all_to_all | solution.py:20
  77.9 7.3 %all-to-all-done.2 = bf16[32,4,128]{2,1,0:T(4,128)(2,1)S(1)} async-done(((bf16[32,4,128]{2,1,0:T(4,128)(2,1)}), bf16[32,4,128]{2,1,0:T(4,128)(2,1)S(1)}, u32[]{:S(2)}, u32[]{:S(2)}) %all-to-all-start.2) | async-done | bytes 32800 | tf_op jit(solution)/shard_map/all_to_all | solution.py:20
  85.3 0.1 compare_select_fusion.1.panel
  85.4 2.3 shard_map.78
  87.8 0.1 pad_maximum_fusion.1
  88.0 36.0 %all_to_all.45 = bf16[32,2,1280]{2,1,0:T(2,128)(2,1)S(1)} all-to-all(bf16[32,2,1280]{2,1,0:T(2,128)(2,1)S(1)} %pad_maximum_fusion.1), channel_id=1, replica_groups=mesh['clu'=32,'mem'=32] {'mem'}, dimensions={0} | all-to-all | bytes 327680 | tf_op jit(solution)/shard_map/all_to_all | solution.py:20
  124.0 0.6 copy-done.4
  124.6 0.1 compare_select_fusion.panel
  124.7 1.5 shard_map.79
  126.2 0.7 copy-done.1
  126.9 5.7 %all-to-all-start.4 = ((f32[32,16,128]{2,1,0:T(8,128)}), f32[32,16,128]{2,1,0:T(8,128)S(1)}, u32[]{:S(2)}, u32[]{:S(2)}) async-start(f32[32,16,128]{2,1,0:T(8,128)} %copy-done.1), calls=%async_computation.4 | async-start | bytes 524288 | tf_op jit(solution)/shard_map/all_to_all | solution.py:20
  132.6 1.1 convert_reduce_fusion.2
  133.7 7.9 %all-to-all-done.4.from_cols = f32[32,16,128]{2,1,0:T(8,128)S(1)} async-done(((f32[32,16,128]{2,1,0:T(8,128)}), f32[32,16,128]{2,1,0:T(8,128)S(1)}, u32[]{:S(2)}, u32[]{:S(2)}) %all-to-all-start.4) | async-done | bytes 262176 | tf_op jit(solution)/shard_map/all_to_all | solution.py:20
  141.6 0.7 shard_map.80
  142.3 3.8 %all-to-all-start.5 = ((bf16[32,16,128]{2,1,0:T(8,128)(2,1)}), bf16[32,16,128]{2,1,0:T(8,128)(2,1)S(1)}, u32[]{:S(2)}, u32[]{:S(2)}) async-start(bf16[32,16,128]{2,1,0:T(8,128)(2,1)} %get-tuple-element.20), calls=%async_computation.5 | async-start | bytes 262144 | tf_op jit(solution)/shard_map/all_to_all | solution.py:20
  146.1 0.1 eq.116
  146.2 7.6 %all-to-all-done.5.panel = bf16[32,16,128]{2,1,0:T(8,128)(2,1)S(1)} async-done(((bf16[32,16,128]{2,1,0:T(8,128)(2,1)}), bf16[32,16,128]{2,1,0:T(8,128)(2,1)S(1)}, u32[]{:S(2)}, u32[]{:S(2)}) %all-to-all-start.5) | async-done | bytes 131104 | tf_op jit(solution)/shard_map/all_to_all | solution.py:20
  153.8 3.9 %all-to-all-start.6 = ((bf16[32,16,128]{2,1,0:T(8,128)(2,1)}), bf16[32,16,128]{2,1,0:T(8,128)(2,1)S(1)}, u32[]{:S(2)}, u32[]{:S(2)}) async-start(bf16[32,16,128]{2,1,0:T(8,128)(2,1)} %get-tuple-element.20), calls=%async_computation.6 | async-start | bytes 262144 | tf_op jit(solution)/shard_map/all_to_all | solution.py:20
  157.7 0.5 iota_compare_fusion.1
  158.2 0.1 fusion.8
  158.3 0.2 fusion.26
  158.5 0.1 reduce_sum.144
  158.6 0.1 reduce_sum.147
  158.7 0.1 reduce-precision_convert_fusion.5
  158.8 0.1 fusion.32
  158.9 0.5 pad.21
  159.4 2.3 shard_map.81
  161.8 0.7 broadcast_in_dim.118
  162.4 0.8 pad_maximum_fusion.2
  163.2 24.6 %all-to-all-done.6.panel = bf16[32,16,128]{2,1,0:T(8,128)(2,1)S(1)} async-done(((bf16[32,16,128]{2,1,0:T(8,128)(2,1)}), bf16[32,16,128]{2,1,0:T(8,128)(2,1)S(1)}, u32[]{:S(2)}, u32[]{:S(2)}) %all-to-all-start.6) | async-done | bytes 131104 | tf_op jit(solution)/shard_map/all_to_all | solution.py:20
  187.8 0.2 multiply_reduce_fusion
  187.9 0.1 reduce_sum.150
  188.1 0.1 select_maximum_fusion.2
  188.1 1.4 fusion.4
  189.5 4.6 %all-to-all-start.7 = ((bf16[32,2,1152]{2,1,0:T(2,128)(2,1)}), bf16[32,2,1152]{2,1,0:T(2,128)(2,1)}, u32[]{:S(2)}, u32[]{:S(2)}) async-start(bf16[32,2,1152]{2,1,0:T(2,128)(2,1)} %fusion.4), calls=%async_computation.7 | async-start | bytes 294912 | tf_op jit(solution)/shard_map/all_to_all | solution.py:20
  194.1 1.5 shard_map.82
  195.6 26.6 %all-to-all-done.7 = bf16[32,2,1152]{2,1,0:T(2,128)(2,1)} async-done(((bf16[32,2,1152]{2,1,0:T(2,128)(2,1)}), bf16[32,2,1152]{2,1,0:T(2,128)(2,1)}, u32[]{:S(2)}, u32[]{:S(2)}) %all-to-all-start.7) | async-done | bytes 147488 | tf_op jit(solution)/shard_map/all_to_all | solution.py:20
  222.3 1.0 convert_reduce_fusion.3
  223.4 0.1 reshape.201
  223.5 0.1 reshape.202
  223.6 0.1 reduce-precision_convert_fusion.1
  223.7 0.1 fusion.31
  223.8 0.7 pad_maximum_fusion
  224.5 9.0 %all-to-all-start.8 = ((bf16[32,24,128]{2,1,0:T(8,128)(2,1)}), bf16[32,24,128]{2,1,0:T(8,128)(2,1)S(1)}, u32[]{:S(2)}, u32[]{:S(2)}) async-start(bf16[32,24,128]{2,1,0:T(8,128)(2,1)} %pad_maximum_fusion), calls=%async_computation.8 | async-start | bytes 393216 | tf_op jit(solution)/shard_map/all_to_all | solution.py:20
  233.6 8.4 %all-to-all-done.8 = bf16[32,24,128]{2,1,0:T(8,128)(2,1)S(1)} async-done(((bf16[32,24,128]{2,1,0:T(8,128)(2,1)}), bf16[32,24,128]{2,1,0:T(8,128)(2,1)S(1)}, u32[]{:S(2)}, u32[]{:S(2)}) %all-to-all-start.8) | async-done | bytes 196640 | tf_op jit(solution)/shard_map/all_to_all | solution.py:20
  242.0 0.1 reshape.204
  242.1 0.1 subtract_divide_fusion.1
  242.2 0.1 broadcast_multiply_fusion
  242.2 1.4 fusion.18
  (49 shorter events, 0.7 us)
Async XLA Ops:
  0.6 22.3 %copy-start = (bf16[1,1,96,128,128]{4,3,2,1,0:T(8,128)(2,1)S(1)}, bf16[1,1,96,128,128]{4,3,2,1,0:T(8,128)(2,1)}, u32[]{:S(2)}) copy-start(bf16[1,1,96,128,128]{4,3,2,1,0:T(8,128)(2,1)} %param.8) | copy-start | bytes 9437188
  0.6 3.8 %copy-start.2 = (s32[1,1,96]{2,1,0:T(1,128)S(1)}, s32[1,1,96]{2,1,0:T(1,128)}, u32[]{:S(2)}) copy-start(s32[1,1,96]{2,1,0:T(1,128)} %param.10) | copy-start | bytes 1156
  0.7 22.3 %copy-start.3 = (s32[1,1,96]{2,1,0:T(1,128)S(1)}, s32[1,1,96]{2,1,0:T(1,128)}, u32[]{:S(2)}) copy-start(s32[1,1,96]{2,1,0:T(1,128)} %param.9) | copy-start | bytes 1156
  1.5 48.2 %copy-start.6 = (s32[256]{0:T(256)S(1)}, s32[256]{0:T(256)}, u32[]{:S(2)}) copy-start(s32[256]{0:T(256)} %param.6) | copy-start | bytes 3076
  1.5 70.1 %copy-start.5 = (f32[256]{0:T(256)S(1)}, f32[256]{0:T(256)}, u32[]{:S(2)}) copy-start(f32[256]{0:T(256)} %param.7) | copy-start | bytes 3076
  5.3 25.0 %all-to-all-start = ((f32[32,2,128]{2,1,0:T(2,128)}), f32[32,2,128]{2,1,0:T(2,128)S(1)}, u32[]{:S(2)}, u32[]{:S(2)}) async-start(f32[32,2,128]{2,1,0:T(2,128)} %copy.8), calls=%async_computation | async-start | bytes 65536 | tf_op jit(solution)/shard_map/all_to_all | solution.py:20
  30.3 41.3 %all-to-all-start.1 = ((f32[32,2,128]{2,1,0:T(2,128)}), f32[32,2,128]{2,1,0:T(2,128)S(1)}, u32[]{:S(2)}, u32[]{:S(2)}) async-start(f32[32,2,128]{2,1,0:T(2,128)} %bitcast.6), calls=%async_computation.1 | async-start | bytes 65536 | tf_op jit(solution)/shard_map/all_to_all | solution.py:20
  71.6 61.0 %copy-start.7 = (f32[2,128]{1,0:T(2,128)}, f32[2,128]{1,0:T(2,128)S(1)}, u32[]{:S(2)}) copy-start(f32[2,128]{1,0:T(2,128)S(1)} %get-tuple-element.38) | copy-start | bytes 3076
  72.3 13.0 %all-to-all-start.2 = ((bf16[32,4,128]{2,1,0:T(4,128)(2,1)}), bf16[32,4,128]{2,1,0:T(4,128)(2,1)S(1)}, u32[]{:S(2)}, u32[]{:S(2)}) async-start(bf16[32,4,128]{2,1,0:T(4,128)(2,1)} %broadcast_in_dim.103), calls=%async_computation.2 | async-start | bytes 65536 | tf_op jit(solution)/shard_map/all_to_all | solution.py:20
  123.9 0.7 copy-start.4
  126.2 0.7 copy-start.1
  126.9 14.7 %all-to-all-start.4 = ((f32[32,16,128]{2,1,0:T(8,128)}), f32[32,16,128]{2,1,0:T(8,128)S(1)}, u32[]{:S(2)}, u32[]{:S(2)}) async-start(f32[32,16,128]{2,1,0:T(8,128)} %copy-done.1), calls=%async_computation.4 | async-start | bytes 524288 | tf_op jit(solution)/shard_map/all_to_all | solution.py:20
  142.3 11.5 %all-to-all-start.5 = ((bf16[32,16,128]{2,1,0:T(8,128)(2,1)}), bf16[32,16,128]{2,1,0:T(8,128)(2,1)S(1)}, u32[]{:S(2)}, u32[]{:S(2)}) async-start(bf16[32,16,128]{2,1,0:T(8,128)(2,1)} %get-tuple-element.20), calls=%async_computation.5 | async-start | bytes 262144 | tf_op jit(solution)/shard_map/all_to_all | solution.py:20
  153.8 34.0 %all-to-all-start.6 = ((bf16[32,16,128]{2,1,0:T(8,128)(2,1)}), bf16[32,16,128]{2,1,0:T(8,128)(2,1)S(1)}, u32[]{:S(2)}, u32[]{:S(2)}) async-start(bf16[32,16,128]{2,1,0:T(8,128)(2,1)} %get-tuple-element.20), calls=%async_computation.6 | async-start | bytes 262144 | tf_op jit(solution)/shard_map/all_to_all | solution.py:20
  189.5 32.7 %all-to-all-start.7 = ((bf16[32,2,1152]{2,1,0:T(2,128)(2,1)}), bf16[32,2,1152]{2,1,0:T(2,128)(2,1)}, u32[]{:S(2)}, u32[]{:S(2)}) async-start(bf16[32,2,1152]{2,1,0:T(2,128)(2,1)} %fusion.4), calls=%async_computation.7 | async-start | bytes 294912 | tf_op jit(solution)/shard_map/all_to_all | solution.py:20
  224.5 17.4 %all-to-all-start.8 = ((bf16[32,24,128]{2,1,0:T(8,128)(2,1)}), bf16[32,24,128]{2,1,0:T(8,128)(2,1)S(1)}, u32[]{:S(2)}, u32[]{:S(2)}) async-start(bf16[32,24,128]{2,1,0:T(8,128)(2,1)} %pad_maximum_fusion), calls=%async_computation.8 | async-start | bytes 393216 | tf_op jit(solution)/shard_map/all_to_all | solution.py:20

commit v4 on v3

--- a/solution.py
+++ b/solution.py
@@ -14,6 +14,8 @@
 BF16 = jnp.bfloat16
 STEP = 32
 LIMIT = 8
+KIND_AT = 3 * NB_DEV
+SUMS_AT = KIND_AT + NB_DEV
 
 
 def swap(parts, axis):
@@ -51,6 +53,33 @@
     out[...] = acc[...].reshape(out.shape).astype(out.dtype)
 
 
+def first_kernel(into_ref, count_ref, from_ref, got, tiles_ref, out, root, acc, wide, known, value):
+    n_clu = got.shape[0]
+    blocks = NB_DEV * n_clu
+    known[...] = got[:, blocks:].astype(F32)
+    totals = jnp.sum(got[:, :blocks].astype(F32), axis=0)
+
+    def whole(row):
+        return known[:, row, :] + known[:, row + NB_DEV, :] + known[:, row + 2 * NB_DEV, :]
+
+    for b in range(NB_DEV):
+        part = slice(b * n_clu, (b + 1) * n_clu)
+        root[part] = lax.rsqrt(1.0 + totals[part] + whole(SUMS_AT + b))
+        value[part] = root[part] * whole(b)
+    for b in range(NB_DEV):
+        for peer in range(n_clu):
+            block = b * n_clu + peer
+            row = (CLASSES, value.shape[1])
+            kind = jnp.broadcast_to(known[peer, KIND_AT + b : KIND_AT + b + 1, :], row)
+            here = jnp.broadcast_to(value[block : block + 1, :], row)
+            classes_now = lax.broadcasted_iota(jnp.int32, row, 0).astype(F32)
+            wide[block] = jnp.where(kind == classes_now, here, 0.0)
+    sum_slots(
+        into_ref, count_ref, tiles_ref, acc, lambda slot: wide[from_ref[slot]].astype(BF16), 1
+    )
+    out[...] = acc[...].reshape(out.shape).astype(out.dtype)
+
+
 def middle_kernel(from_cols, row_image, scale, first, sent):
     scale = scale[...]
     image = scale * (jnp.sum(from_cols[...], axis=0) + row_image[...])
@@ -65,7 +94,7 @@
     return pl.pallas_call(
         kernel,
         in_specs=[smem] * len(index) + [vmem] * (len(panels) + 1),
-        out_specs=vmem,
+        out_specs=jax.tree.map(lambda _: vmem, out),
         scratch_shapes=[pltpu.VMEM(x, F32) for x in scratch],
         out_shape=out,
         compiler_params=pltpu.CompilerParams(vmem_limit_bytes=limit << 20),
@@ -90,33 +119,42 @@
     shape = jax.ShapeDtypeStruct
 
     used = jnp.arange(slots, dtype=jnp.int32) < count
-    blocks = jnp.arange(col_blocks, dtype=jnp.int32)[:, None]
-    col_table = ((cols[None, :] == blocks) & used).astype(F32)
-    col_totals = jnp.sum(tiles, axis=1, dtype=F32)
-    col_part = jnp.einsum("kt,tj->kj", col_table, col_totals, precision=lax.Precision.HIGHEST)
-    row_part = call_on_tiles(
-        functools.partial(totals_kernel, 1), (rows, count), (), tiles,
-        shape((row_blocks, side), F32), (row_space,), LIMIT,
-    )
-    from_cols = swap(col_part.reshape(n_clu, NB_DEV, side), "clu")
-    row_part, from_cols = lax.optimization_barrier((row_part, from_cols))
+    blocks = jnp.arange(row_blocks, dtype=jnp.int32)[:, None]
+    row_table = ((rows[None, :] == blocks) & used).astype(F32)
+    row_totals = jnp.sum(tiles, axis=2, dtype=F32)
+    row_part = jnp.einsum("rt,ti->ri", row_table, row_totals, precision=lax.Precision.HIGHEST)
     from_rows = swap(row_part.reshape(n_mem, NB_DEV, side), "mem")
-    degree = 1.0 + jnp.sum(from_cols, axis=0) + jnp.sum(from_rows, axis=0)
-    inverse_root = lax.rsqrt(degree)
+    cols_by_half = cols % NB_DEV * n_clu + cols // NB_DEV
+    col_part = call_on_tiles(
+        functools.partial(totals_kernel, 0), (cols_by_half, count), (), tiles,
+        shape((col_blocks, side), F32), (col_space,), LIMIT,
+    )
 
     kinds = seed_class.reshape(NB_DEV, side)
     weight = seed_weight.reshape(NB_DEV, side)
-    own = jnp.concatenate([inverse_root * weight, kinds.astype(F32)])
+    known = jnp.concatenate([col_part.astype(BF16), split3(weight), kinds.astype(BF16)])
+    classes_now = jnp.arange(CLASSES, dtype=jnp.int32)[:, None]
+    labels = jnp.where(kinds[:, None] == classes_now, weight[:, None], jnp.float32(0.0))
+    known, labels, from_rows = lax.optimization_barrier((known, labels, from_rows))
+    sent = jnp.concatenate([known, split3(jnp.sum(from_rows, axis=0))])
+    sent = jnp.pad(sent, ((0, -sent.shape[0] % 16), (0, 0)))
+    got = swap(jnp.broadcast_to(sent[None], (n_clu,) + sent.shape), "clu")
+
+    row_sum, col_root = call_on_tiles(
+        first_kernel, (rows, count, cols_by_half), (got,), tiles,
+        (shape((n_mem, height, side), BF16), shape((col_blocks, side), F32)),
+        (row_space, col_space, (n_clu, got.shape[1] - col_blocks, side), (col_blocks, side)), LIMIT,
+    )
+    inverse_root = lax.dynamic_index_in_dim(
+        col_root.reshape(NB_DEV, n_clu, side), lax.axis_index("clu"), 1, keepdims=False
+    )
+    own = jnp.concatenate([inverse_root * weight, kinds.astype(F32)], axis=1)
     peers = max(n_mem, n_clu)
-    col_own = swap(jnp.broadcast_to(own.astype(BF16)[None], (n_clu,) + own.shape), "clu")
-    classes_now = jnp.arange(CLASSES, dtype=jnp.int32)[:, None]
-
     def panel_of(value, kind):
         kind = kind.reshape(-1, 1, side)
         panel = jnp.where(kind == classes_now.astype(BF16), value.reshape(-1, 1, side), jnp.zeros((), BF16))
         return panel.reshape(-1, height, side)
 
-    labels = jnp.where(kinds[:, None] == classes_now, weight[:, None], jnp.float32(0.0))
     scale = inverse_root[:, None]
 
     def forward(col_panel):
@@ -144,8 +182,7 @@
     def narrow(image):
         return image[:, :lanes].reshape(NB_DEV, CLASSES, side)
 
-    row_sum = forward(panel_of(col_own[:, :NB_DEV], col_own[:, NB_DEV:]))
-    from_mem = swap(wide(row_sum, jnp.concatenate([own[:NB_DEV], own[NB_DEV:]], axis=1)), "mem")
+    from_mem = swap(wide(row_sum, own), "mem")
     col_sum = backward(
         panel_of(from_mem[:, :, lanes : lanes + side], from_mem[:, :, lanes + side :]), F32
     )

time: 244 us -> 241 us (0.988)
  waiting for transfers between devices: 109 us -> 134 us
  blocking collectives: 36 us -> 11.5 us
  starting transfers between devices: 69.5 us -> 65.6 us
    all_to_all x8 -> x7, waiting for transfers between devices: 109 us -> 134 us  [swap(): return lax.all_to_all(parts, axis, 0, 0, tiled=True)]
    all_to_all x1, blocking collectives: 36 us -> 11.5 us  [swap(): return lax.all_to_all(parts, axis, 0, 0, tiled=True)]
    all_to_all x8 -> x7, starting transfers between devices: 69.5 us -> 65.6 us  [swap(): return lax.all_to_all(parts, axis, 0, 0, tiled=True)]
  transfers between devices with their start and end apart: 8 -> 7, of which waited for: 8 -> 7; matrix products, arithmetic and copies ran while one was open for 2% -> 2% of each run, Pallas kernels for 3% -> 2%
where the time goes in v4:
time: 241 us; the launch traced here: 240 us
  waiting for transfers between devices  134 us (56%)
  starting transfers between devices  65.6 us (27%)
  other arithmetic  12 us (5%)
  blocking collectives  11.5 us (5%)
  Pallas kernels  10.6 us (4%)
  local copies, waits for them, and re-layouts  4.2 us (2%)
    all_to_all x7, waiting for transfers between devices, swap(): return lax.all_to_all(parts, axis, 0, 0, tiled=True)  134 us
    all_to_all x7, starting transfers between devices, swap(): return lax.all_to_all(parts, axis, 0, 0, tiled=True)  65.6 us
    all_to_all x1, blocking collectives, swap(): return lax.all_to_all(parts, axis, 0, 0, tiled=True)  11.5 us
    pallas_call x5, Pallas kernels, call_on_tiles(): pl.pallas_call(kernel, in_specs=[smem] * len(index) + [vmem] * (len(panel...  9.94 us
  transfers between devices with their start and end apart: 7, of which 7 were waited for; matrix products, arithmetic and copies ran while one was open for 2% of the time, Pallas kernels for 2%

profile of v4, /device:TPU:1, one launch (start us, length us, event | category | flops | bytes accessed | tf_op | source)
XLA Modules:
  0.0 239.8 jit_solution(17181142029382886560)
XLA Ops:
  0.6 0.0 copy-start
  0.6 0.0 copy-start.2
  0.7 0.0 copy-start.8
  0.7 0.0 copy-start.9
  0.7 0.0 copy-start.3
  1.5 2.9 %convert_reduce_fusion = f32[96,128]{1,0:T(8,128)S(1)} fusion(bf16[1,1,96,128,128]{4,3,2,1,0:T(8,128)(2,1)} %param.8), kind=kLoop, calls=%fused_computation | loop fusion | flops 3133440 | bytes 3194880 | tf_op jit(solution)/shard_map/reduce_sum | solution.py:124
  4.4 0.0 copy-done.2
  4.5 0.2 fusion
  4.7 0.6 copy.8
  5.3 29.3 %all-to-all-start = ((f32[32,2,128]{2,1,0:T(2,128)}), f32[32,2,128]{2,1,0:T(2,128)S(1)}, u32[]{:S(2)}, u32[]{:S(2)}) async-start(f32[32,2,128]{2,1,0:T(2,128)} %copy.8), calls=%async_computation | async-start | bytes 65536 | tf_op jit(solution)/shard_map/all_to_all | solution.py:22
  34.6 0.0 copy-done.8
  34.6 0.0 copy-done.9
  34.7 1.5 shard_map.77
  36.2 20.3 %all-to-all-done = f32[32,2,128]{2,1,0:T(2,128)S(1)} async-done(((f32[32,2,128]{2,1,0:T(2,128)}), f32[32,2,128]{2,1,0:T(2,128)S(1)}, u32[]{:S(2)}, u32[]{:S(2)}) %all-to-all-start) | async-done | bytes 32800 | tf_op jit(solution)/shard_map/all_to_all | solution.py:22
  56.6 0.9 broadcast_in_dim.56
  57.6 9.2 %all-to-all-start.1 = ((bf16[32,80,128]{2,1,0:T(8,128)(2,1)}), bf16[32,80,128]{2,1,0:T(8,128)(2,1)}, u32[]{:S(2)}, u32[]{:S(2)}) async-start(bf16[32,80,128]{2,1,0:T(8,128)(2,1)} %broadcast_in_dim.56), calls=%async_computation.1 | async-start | bytes 1310720 | tf_op jit(solution)/shard_map/all_to_all | solution.py:22
  66.8 13.0 %all-to-all-done.1.got = bf16[32,80,128]{2,1,0:T(8,128)(2,1)} async-done(((bf16[32,80,128]{2,1,0:T(8,128)(2,1)}), bf16[32,80,128]{2,1,0:T(8,128)(2,1)}, u32[]{:S(2)}, u32[]{:S(2)}) %all-to-all-start.1) | async-done | bytes 655392 | tf_op jit(solution)/shard_map/all_to_all | solution.py:22
  79.8 3.1 %shard_map.78 = (bf16[32,16,128]{2,1,0:T(8,128)(2,1)S(1)}, f32[64,128]{1,0:T(8,128)S(1)}) custom-call(s32[96]{0:T(128)S(1)} %bitcast.104, s32[1]{0:T(128)} %bitcast.93.count_ref, s32[96]{0:T(128)S(1)} %fusion.36.into_ref.from_ref, bf16[32,80,128]{2,1,0:T(8,128)(2,1)} %all-to-all-done.1.got, bf16[96,128,128]{2,1,0:T(8,128)(2,1)S(1)} %bitcast.99), custom_call_target="tpu_custom_call" | custom-call | flops 25165824 | bytes 3145728 | tf_op jit(solution)/shard_map/pallas_call | solution.py:94
  83.0 0.8 pad_maximum_fusion.1
  83.8 3.9 %all-to-all-start.2 = ((bf16[32,2,1280]{2,1,0:T(2,128)(2,1)}), bf16[32,2,1280]{2,1,0:T(2,128)(2,1)S(1)}, u32[]{:S(2)}, u32[]{:S(2)}) async-start(bf16[32,2,1280]{2,1,0:T(2,128)(2,1)} %pad_maximum_fusion.1), calls=%async_computation.2 | async-start | bytes 327680 | tf_op jit(solution)/shard_map/all_to_all | solution.py:22
  87.7 0.1 eq.76
  87.8 32.8 %all-to-all-done.2 = bf16[32,2,1280]{2,1,0:T(2,128)(2,1)S(1)} async-done(((bf16[32,2,1280]{2,1,0:T(2,128)(2,1)}), bf16[32,2,1280]{2,1,0:T(2,128)(2,1)S(1)}, u32[]{:S(2)}, u32[]{:S(2)}) %all-to-all-start.2) | async-done | bytes 163872 | tf_op jit(solution)/shard_map/all_to_all | solution.py:22
  120.7 0.1 compare_select_fusion.panel
  120.8 1.5 shard_map.79
  122.3 0.7 copy-done.1
  123.0 5.8 %all-to-all-start.3 = ((f32[32,16,128]{2,1,0:T(8,128)}), f32[32,16,128]{2,1,0:T(8,128)S(1)}, u32[]{:S(2)}, u32[]{:S(2)}) async-start(f32[32,16,128]{2,1,0:T(8,128)} %copy-done.1), calls=%async_computation.3 | async-start | bytes 524288 | tf_op jit(solution)/shard_map/all_to_all | solution.py:22
  128.8 1.1 convert_reduce_fusion.2
  129.9 0.0 copy-done.7
  129.9 7.9 %all-to-all-done.3.from_cols = f32[32,16,128]{2,1,0:T(8,128)S(1)} async-done(((f32[32,16,128]{2,1,0:T(8,128)}), f32[32,16,128]{2,1,0:T(8,128)S(1)}, u32[]{:S(2)}, u32[]{:S(2)}) %all-to-all-start.3) | async-done | bytes 262176 | tf_op jit(solution)/shard_map/all_to_all | solution.py:22
  137.8 0.7 shard_map.80
  138.5 11.5 %all_to_all.40.panel = bf16[32,16,128]{2,1,0:T(8,128)(2,1)S(1)} all-to-all(bf16[32,16,128]{2,1,0:T(8,128)(2,1)} %get-tuple-element.26), channel_id=1, replica_groups=mesh['clu'=32,'mem'=32] {'clu'}, dimensions={0} | all-to-all | bytes 262144 | tf_op jit(solution)/shard_map/all_to_all | solution.py:22
  150.0 3.9 %all-to-all-start.5 = ((bf16[32,16,128]{2,1,0:T(8,128)(2,1)}), bf16[32,16,128]{2,1,0:T(8,128)(2,1)S(1)}, u32[]{:S(2)}, u32[]{:S(2)}) async-start(bf16[32,16,128]{2,1,0:T(8,128)(2,1)} %get-tuple-element.26), calls=%async_computation.5 | async-start | bytes 262144 | tf_op jit(solution)/shard_map/all_to_all | solution.py:22
  153.8 0.5 iota_compare_fusion.2
  154.4 0.1 multiply_reduce_fusion.1
  154.5 0.1 reduce_sum.128
  154.6 0.0 copy-done.5
  154.6 0.1 multiply_reduce_fusion.2
  154.7 0.1 reduce-precision_convert_fusion.9
  154.8 0.1 fusion.38
  154.9 0.5 pad.26
  155.4 2.3 shard_map.81
  157.8 0.6 broadcast_in_dim.98
  158.3 0.8 pad_maximum_fusion.2
  159.1 24.8 %all-to-all-done.5.panel = bf16[32,16,128]{2,1,0:T(8,128)(2,1)S(1)} async-done(((bf16[32,16,128]{2,1,0:T(8,128)(2,1)}), bf16[32,16,128]{2,1,0:T(8,128)(2,1)S(1)}, u32[]{:S(2)}, u32[]{:S(2)}) %all-to-all-start.5) | async-done | bytes 131104 | tf_op jit(solution)/shard_map/all_to_all | solution.py:22
  183.9 0.2 multiply_reduce_fusion
  184.1 0.1 reduce_sum.131
  184.2 0.1 select_maximum_fusion.2
  184.3 1.4 fusion.11
  185.7 4.6 %all-to-all-start.6 = ((bf16[32,2,1152]{2,1,0:T(2,128)(2,1)}), bf16[32,2,1152]{2,1,0:T(2,128)(2,1)}, u32[]{:S(2)}, u32[]{:S(2)}) async-start(bf16[32,2,1152]{2,1,0:T(2,128)(2,1)} %fusion.11), calls=%async_computation.6 | async-start | bytes 294912 | tf_op jit(solution)/shard_map/all_to_all | solution.py:22
  190.3 1.5 shard_map.82
  191.8 26.6 %all-to-all-done.6 = bf16[32,2,1152]{2,1,0:T(2,128)(2,1)} async-done(((bf16[32,2,1152]{2,1,0:T(2,128)(2,1)}), bf16[32,2,1152]{2,1,0:T(2,128)(2,1)}, u32[]{:S(2)}, u32[]{:S(2)}) %all-to-all-start.6) | async-done | bytes 147488 | tf_op jit(solution)/shard_map/all_to_all | solution.py:22
  218.4 1.0 convert_reduce_fusion.3
  219.5 0.1 reshape.170
  219.6 0.1 reshape.171
  219.7 0.1 reduce-precision_convert_fusion.5
  219.8 0.1 fusion.37
  219.9 0.7 pad_maximum_fusion
  220.6 9.0 %all-to-all-start.7 = ((bf16[32,24,128]{2,1,0:T(8,128)(2,1)}), bf16[32,24,128]{2,1,0:T(8,128)(2,1)S(1)}, u32[]{:S(2)}, u32[]{:S(2)}) async-start(bf16[32,24,128]{2,1,0:T(8,128)(2,1)} %pad_maximum_fusion), calls=%async_computation.7 | async-start | bytes 393216 | tf_op jit(solution)/shard_map/all_to_all | solution.py:22
  229.7 8.4 %all-to-all-done.7 = bf16[32,24,128]{2,1,0:T(8,128)(2,1)S(1)} async-done(((bf16[32,24,128]{2,1,0:T(8,128)(2,1)}), bf16[32,24,128]{2,1,0:T(8,128)(2,1)S(1)}, u32[]{:S(2)}, u32[]{:S(2)}) %all-to-all-start.7) | async-done | bytes 196640 | tf_op jit(solution)/shard_map/all_to_all | solution.py:22
  238.1 0.1 reshape.173
  238.2 0.1 subtract_divide_fusion.1
  238.3 0.1 broadcast_multiply_fusion
  238.4 0.0 copy-done.6
  238.4 1.4 fusion.24
  (49 shorter events, 0.7 us)
Async XLA Ops:
  0.6 34.0 %copy-start = (bf16[1,1,96,128,128]{4,3,2,1,0:T(8,128)(2,1)S(1)}, bf16[1,1,96,128,128]{4,3,2,1,0:T(8,128)(2,1)}, u32[]{:S(2)}) copy-start(bf16[1,1,96,128,128]{4,3,2,1,0:T(8,128)(2,1)} %param.8) | copy-start | bytes 9437188
  0.6 3.8 %copy-start.2 = (s32[1,1,96]{2,1,0:T(1,128)S(1)}, s32[1,1,96]{2,1,0:T(1,128)}, u32[]{:S(2)}) copy-start(s32[1,1,96]{2,1,0:T(1,128)} %param.9) | copy-start | bytes 1156
  0.7 33.9 %copy-start.8 = (f32[256]{0:T(256)S(1)}, f32[256]{0:T(256)}, u32[]{:S(2)}) copy-start(f32[256]{0:T(256)} %param.7) | copy-start | bytes 3076
  0.7 33.9 %copy-start.9 = (s32[256]{0:T(256)S(1)}, s32[256]{0:T(256)}, u32[]{:S(2)}) copy-start(s32[256]{0:T(256)} %param.6) | copy-start | bytes 3076
  0.7 34.0 %copy-start.3 = (s32[1,1,96]{2,1,0:T(1,128)S(1)}, s32[1,1,96]{2,1,0:T(1,128)}, u32[]{:S(2)}) copy-start(s32[1,1,96]{2,1,0:T(1,128)} %param.10) | copy-start | bytes 1156
  5.3 51.3 %all-to-all-start = ((f32[32,2,128]{2,1,0:T(2,128)}), f32[32,2,128]{2,1,0:T(2,128)S(1)}, u32[]{:S(2)}, u32[]{:S(2)}) async-start(f32[32,2,128]{2,1,0:T(2,128)} %copy.8), calls=%async_computation | async-start | bytes 65536 | tf_op jit(solution)/shard_map/all_to_all | solution.py:22
  36.2 118.3 %copy-start.5 = (f32[2,8,128]{2,1,0:T(8,128)}, f32[2,8,128]{2,1,0:T(8,128)S(1)}, u32[]{:S(2)}) copy-start(f32[2,8,128]{2,1,0:T(8,128)S(1)} %fusion.29) | copy-start | bytes 24580
  57.6 22.2 %all-to-all-start.1 = ((bf16[32,80,128]{2,1,0:T(8,128)(2,1)}), bf16[32,80,128]{2,1,0:T(8,128)(2,1)}, u32[]{:S(2)}, u32[]{:S(2)}) async-start(bf16[32,80,128]{2,1,0:T(8,128)(2,1)} %broadcast_in_dim.56), calls=%async_computation.1 | async-start | bytes 1310720 | tf_op jit(solution)/shard_map/all_to_all | solution.py:22
  82.9 46.9 %copy-start.7 = (f32[2,1,128]{2,1,0:T(1,128)}, f32[2,1,128]{2,1,0:T(1,128)S(1)}, u32[]{:S(2)}) copy-start(f32[2,1,128]{2,1,0:T(1,128)S(1)} %constant_dynamic-slice_fusion) | copy-start | bytes 3076
  83.8 36.8 %all-to-all-start.2 = ((bf16[32,2,1280]{2,1,0:T(2,128)(2,1)}), bf16[32,2,1280]{2,1,0:T(2,128)(2,1)S(1)}, u32[]{:S(2)}, u32[]{:S(2)}) async-start(bf16[32,2,1280]{2,1,0:T(2,128)(2,1)} %pad_maximum_fusion.1), calls=%async_computation.2 | async-start | bytes 327680 | tf_op jit(solution)/shard_map/all_to_all | solution.py:22
  120.6 2.4 %copy-start.4 = (bf16[32,2,1280]{2,1,0:T(2,128)(2,1)}, bf16[32,2,1280]{2,1,0:T(2,128)(2,1)S(1)}, u32[]{:S(2)}) copy-start(bf16[32,2,1280]{2,1,0:T(2,128)(2,1)S(1)} %all-to-all-done.2) | copy-start | bytes 491524
  122.3 0.7 copy-start.1
  123.0 14.8 %all-to-all-start.3 = ((f32[32,16,128]{2,1,0:T(8,128)}), f32[32,16,128]{2,1,0:T(8,128)S(1)}, u32[]{:S(2)}, u32[]{:S(2)}) async-start(f32[32,16,128]{2,1,0:T(8,128)} %copy-done.1), calls=%async_computation.3 | async-start | bytes 524288 | tf_op jit(solution)/shard_map/all_to_all | solution.py:22
  150.0 34.0 %all-to-all-start.5 = ((bf16[32,16,128]{2,1,0:T(8,128)(2,1)}), bf16[32,16,128]{2,1,0:T(8,128)(2,1)S(1)}, u32[]{:S(2)}, u32[]{:S(2)}) async-start(bf16[32,16,128]{2,1,0:T(8,128)(2,1)} %get-tuple-element.26), calls=%async_computation.5 | async-start | bytes 262144 | tf_op jit(solution)/shard_map/all_to_all | solution.py:22
  184.1 54.3 %copy-start.6 = (f32[2,8,128]{2,1,0:T(8,128)S(1)}, f32[2,8,128]{2,1,0:T(8,128)}, u32[]{:S(2)}) copy-start(f32[2,8,128]{2,1,0:T(8,128)} %copy-done.5) | copy-start | bytes 24580
  185.7 32.7 %all-to-all-start.6 = ((bf16[32,2,1152]{2,1,0:T(2,128)(2,1)}), bf16[32,2,1152]{2,1,0:T(2,128)(2,1)}, u32[]{:S(2)}, u32[]{:S(2)}) async-start(bf16[32,2,1152]{2,1,0:T(2,128)(2,1)} %fusion.11), calls=%async_computation.6 | async-start | bytes 294912 | tf_op jit(solution)/shard_map/all_to_all | solution.py:22
  220.6 17.4 %all-to-all-start.7 = ((bf16[32,24,128]{2,1,0:T(8,128)(2,1)}), bf16[32,24,128]{2,1,0:T(8,128)(2,1)S(1)}, u32[]{:S(2)}, u32[]{:S(2)}) async-start(bf16[32,24,128]{2,1,0:T(8,128)(2,1)} %pad_maximum_fusion), calls=%async_computation.7 | async-start | bytes 393216 | tf_op jit(solution)/shard_map/all_to_all | solution.py:22

commit v5 on v4

--- a/solution.py
+++ b/solution.py
@@ -12,7 +12,6 @@
 DAMP = 0.99
 F32 = jnp.float32
 BF16 = jnp.bfloat16
-STEP = 32
 LIMIT = 8
 KIND_AT = 3 * NB_DEV
 SUMS_AT = KIND_AT + NB_DEV
@@ -135,7 +134,8 @@
     known = jnp.concatenate([col_part.astype(BF16), split3(weight), kinds.astype(BF16)])
     classes_now = jnp.arange(CLASSES, dtype=jnp.int32)[:, None]
     labels = jnp.where(kinds[:, None] == classes_now, weight[:, None], jnp.float32(0.0))
-    known, labels, from_rows = lax.optimization_barrier((known, labels, from_rows))
+    table = jnp.broadcast_to(classes_now.astype(BF16), (CLASSES, side))
+    known, labels, table, from_rows = lax.optimization_barrier((known, labels, table, from_rows))
     sent = jnp.concatenate([known, split3(jnp.sum(from_rows, axis=0))])
     sent = jnp.pad(sent, ((0, -sent.shape[0] % 16), (0, 0)))
     got = swap(jnp.broadcast_to(sent[None], (n_clu,) + sent.shape), "clu")
@@ -152,7 +152,7 @@
     peers = max(n_mem, n_clu)
     def panel_of(value, kind):
         kind = kind.reshape(-1, 1, side)
-        panel = jnp.where(kind == classes_now.astype(BF16), value.reshape(-1, 1, side), jnp.zeros((), BF16))
+        panel = jnp.where(kind == table, value.reshape(-1, 1, side), jnp.zeros((), BF16))
         return panel.reshape(-1, height, side)
 
     scale = inverse_root[:, None]

time: 241 us -> 240 us (level)
  blocking collectives: 11.5 us -> 47.4 us
  waiting for transfers between devices: 134 us -> 101 us
  starting transfers between devices: 65.6 us -> 61.8 us
    all_to_all x1 -> x2, blocking collectives: 11.5 us -> 47.4 us  [swap(): return lax.all_to_all(parts, axis, 0, 0, tiled=True)]
    all_to_all x7 -> x6, waiting for transfers between devices: 134 us -> 101 us  [swap(): return lax.all_to_all(parts, axis, 0, 0, tiled=True)]
    all_to_all x7 -> x6, starting transfers between devices: 65.6 us -> 61.8 us  [swap(): return lax.all_to_all(parts, axis, 0, 0, tiled=True)]
  transfers between devices with their start and end apart: 7 -> 6, of which waited for: 7 -> 6; matrix products, arithmetic and copies ran while one was open for 2% -> 2% of each run, Pallas kernels for 2% -> 2%
where the time goes in v5:
time: 240 us; the launch traced here: 239 us
  waiting for transfers between devices  101 us (42%)
  starting transfers between devices  61.8 us (26%)
  blocking collectives  47.4 us (20%)
  other arithmetic  11.3 us (5%)
  Pallas kernels  10.6 us (4%)
  local copies, waits for them, and re-layouts  4.78 us (2%)
    all_to_all x6, waiting for transfers between devices, swap(): return lax.all_to_all(parts, axis, 0, 0, tiled=True)  101 us
    all_to_all x6, starting transfers between devices, swap(): return lax.all_to_all(parts, axis, 0, 0, tiled=True)  61.8 us
    all_to_all x2, blocking collectives, swap(): return lax.all_to_all(parts, axis, 0, 0, tiled=True)  47.4 us
    pallas_call x5, Pallas kernels, call_on_tiles(): pl.pallas_call(kernel, in_specs=[smem] * len(index) + [vmem] * (len(panel...  9.94 us
  transfers between devices with their start and end apart: 6, of which 6 were waited for; matrix products, arithmetic and copies ran while one was open for 2% of the time, Pallas kernels for 2%

profile of v5, /device:TPU:1, one launch (start us, length us, event | category | flops | bytes accessed | tf_op | source)
XLA Modules:
  0.0 238.8 jit_solution(6598202309654710815)
XLA Ops:
  0.6 0.0 copy-start
  0.6 0.0 copy-start.2
  0.7 0.0 copy-start.9
  0.7 0.0 copy-start.3
  0.7 0.0 copy-start.8
  1.5 2.9 %convert_reduce_fusion = f32[96,128]{1,0:T(8,128)S(1)} fusion(bf16[1,1,96,128,128]{4,3,2,1,0:T(8,128)(2,1)} %param.8), kind=kLoop, calls=%fused_computation | loop fusion | flops 3133440 | bytes 3194880 | tf_op jit(solution)/shard_map/reduce_sum | solution.py:123
  4.5 0.0 copy-done.2
  4.5 0.2 fusion
  4.7 0.6 copy.8
  5.3 29.3 %all-to-all-start = ((f32[32,2,128]{2,1,0:T(2,128)}), f32[32,2,128]{2,1,0:T(2,128)S(1)}, u32[]{:S(2)}, u32[]{:S(2)}) async-start(f32[32,2,128]{2,1,0:T(2,128)} %copy.8), calls=%async_computation | async-start | bytes 65536 | tf_op jit(solution)/shard_map/all_to_all | solution.py:21
  34.6 0.0 copy-done.9
  34.6 0.0 copy-done.3
  34.6 0.0 copy-done.8
  34.7 0.0 copy-done
  34.7 1.5 shard_map.77
  36.3 0.0 copy-start.5
  36.3 20.3 %all-to-all-done = f32[32,2,128]{2,1,0:T(2,128)S(1)} async-done(((f32[32,2,128]{2,1,0:T(2,128)}), f32[32,2,128]{2,1,0:T(2,128)S(1)}, u32[]{:S(2)}, u32[]{:S(2)}) %all-to-all-start) | async-done | bytes 32800 | tf_op jit(solution)/shard_map/all_to_all | solution.py:21
  56.6 0.1 broadcast_in_dim.56
  56.7 0.9 broadcast_in_dim.57
  57.7 9.2 %all-to-all-start.1 = ((bf16[32,80,128]{2,1,0:T(8,128)(2,1)}), bf16[32,80,128]{2,1,0:T(8,128)(2,1)}, u32[]{:S(2)}, u32[]{:S(2)}) async-start(bf16[32,80,128]{2,1,0:T(8,128)(2,1)} %broadcast_in_dim.57), calls=%async_computation.1 | async-start | bytes 1310720 | tf_op jit(solution)/shard_map/all_to_all | solution.py:21
  66.9 13.0 %all-to-all-done.1.got = bf16[32,80,128]{2,1,0:T(8,128)(2,1)} async-done(((bf16[32,80,128]{2,1,0:T(8,128)(2,1)}), bf16[32,80,128]{2,1,0:T(8,128)(2,1)}, u32[]{:S(2)}, u32[]{:S(2)}) %all-to-all-start.1) | async-done | bytes 655392 | tf_op jit(solution)/shard_map/all_to_all | solution.py:21
  79.9 3.1 %shard_map.78 = (bf16[32,16,128]{2,1,0:T(8,128)(2,1)S(1)}, f32[64,128]{1,0:T(8,128)S(1)}) custom-call(s32[96]{0:T(128)S(1)} %bitcast.100, s32[1]{0:T(128)} %bitcast.88.count_ref, s32[96]{0:T(128)S(1)} %fusion.36.into_ref.from_ref, bf16[32,80,128]{2,1,0:T(8,128)(2,1)} %all-to-all-done.1.got, bf16[96,128,128]{2,1,0:T(8,128)(2,1)S(1)} %bitcast.94), custom_call_target="tpu_custom_call" | custom-call | flops 25165824 | bytes 3145728 | tf_op jit(solution)/shard_map/pallas_call | solution.py:93
  83.1 0.1 pad_maximum_fusion.1
  83.3 35.9 %all_to_all.40 = bf16[32,2,1280]{2,1,0:T(2,128)(2,1)S(1)} all-to-all(bf16[32,2,1280]{2,1,0:T(2,128)(2,1)S(1)} %pad_maximum_fusion.1), channel_id=1, replica_groups=mesh['clu'=32,'mem'=32] {'mem'}, dimensions={0} | all-to-all | bytes 327680 | tf_op jit(solution)/shard_map/all_to_all | solution.py:21
  119.2 0.6 copy-done.4
  119.9 1.5 shard_map.79
  121.4 0.7 copy-done.1
  122.1 5.8 %all-to-all-start.3 = ((f32[32,16,128]{2,1,0:T(8,128)}), f32[32,16,128]{2,1,0:T(8,128)S(1)}, u32[]{:S(2)}, u32[]{:S(2)}) async-start(f32[32,16,128]{2,1,0:T(8,128)} %copy-done.1), calls=%async_computation.3 | async-start | bytes 524288 | tf_op jit(solution)/shard_map/all_to_all | solution.py:21
  127.9 1.1 convert_reduce_fusion.2
  129.0 7.9 %all-to-all-done.3.from_cols = f32[32,16,128]{2,1,0:T(8,128)S(1)} async-done(((f32[32,16,128]{2,1,0:T(8,128)}), f32[32,16,128]{2,1,0:T(8,128)S(1)}, u32[]{:S(2)}, u32[]{:S(2)}) %all-to-all-start.3) | async-done | bytes 262176 | tf_op jit(solution)/shard_map/all_to_all | solution.py:21
  136.9 0.7 shard_map.80
  137.5 11.5 %all_to_all.41.panel = bf16[32,16,128]{2,1,0:T(8,128)(2,1)S(1)} all-to-all(bf16[32,16,128]{2,1,0:T(8,128)(2,1)} %get-tuple-element.28), channel_id=1, replica_groups=mesh['clu'=32,'mem'=32] {'clu'}, dimensions={0} | all-to-all | bytes 262144 | tf_op jit(solution)/shard_map/all_to_all | solution.py:21
  149.0 3.9 %all-to-all-start.5 = ((bf16[32,16,128]{2,1,0:T(8,128)(2,1)}), bf16[32,16,128]{2,1,0:T(8,128)(2,1)S(1)}, u32[]{:S(2)}, u32[]{:S(2)}) async-start(bf16[32,16,128]{2,1,0:T(8,128)(2,1)} %get-tuple-element.28), calls=%async_computation.5 | async-start | bytes 262144 | tf_op jit(solution)/shard_map/all_to_all | solution.py:21
  152.9 0.5 iota_compare_fusion.2
  153.4 0.1 multiply_reduce_fusion.1
  153.5 0.1 reduce_sum.128
  153.6 0.0 copy-done.5
  153.7 0.1 multiply_reduce_fusion.2
  153.8 0.1 reduce-precision_convert_fusion.9
  153.9 0.1 fusion.38
  154.0 0.5 pad.26
  154.5 2.3 shard_map.81
  156.8 0.6 broadcast_in_dim.101
  157.4 0.8 pad_maximum_fusion.2
  158.2 24.8 %all-to-all-done.5.panel = bf16[32,16,128]{2,1,0:T(8,128)(2,1)S(1)} async-done(((bf16[32,16,128]{2,1,0:T(8,128)(2,1)}), bf16[32,16,128]{2,1,0:T(8,128)(2,1)S(1)}, u32[]{:S(2)}, u32[]{:S(2)}) %all-to-all-start.5) | async-done | bytes 131104 | tf_op jit(solution)/shard_map/all_to_all | solution.py:21
  183.0 0.2 multiply_reduce_fusion
  183.2 0.1 reduce_sum.131
  183.3 0.1 select_maximum_fusion.2
  183.4 1.4 fusion.11
  184.8 4.6 %all-to-all-start.6 = ((bf16[32,2,1152]{2,1,0:T(2,128)(2,1)}), bf16[32,2,1152]{2,1,0:T(2,128)(2,1)}, u32[]{:S(2)}, u32[]{:S(2)}) async-start(bf16[32,2,1152]{2,1,0:T(2,128)(2,1)} %fusion.11), calls=%async_computation.6 | async-start | bytes 294912 | tf_op jit(solution)/shard_map/all_to_all | solution.py:21
  189.3 1.5 shard_map.82
  190.9 26.6 %all-to-all-done.6 = bf16[32,2,1152]{2,1,0:T(2,128)(2,1)} async-done(((bf16[32,2,1152]{2,1,0:T(2,128)(2,1)}), bf16[32,2,1152]{2,1,0:T(2,128)(2,1)}, u32[]{:S(2)}, u32[]{:S(2)}) %all-to-all-start.6) | async-done | bytes 147488 | tf_op jit(solution)/shard_map/all_to_all | solution.py:21
  217.5 1.0 convert_reduce_fusion.3
  218.6 0.1 reshape.173
  218.7 0.1 reshape.172
  218.8 0.1 reduce-precision_convert_fusion.5
  218.9 0.1 fusion.37
  219.0 0.7 pad_maximum_fusion
  219.7 9.0 %all-to-all-start.7 = ((bf16[32,24,128]{2,1,0:T(8,128)(2,1)}), bf16[32,24,128]{2,1,0:T(8,128)(2,1)S(1)}, u32[]{:S(2)}, u32[]{:S(2)}) async-start(bf16[32,24,128]{2,1,0:T(8,128)(2,1)} %pad_maximum_fusion), calls=%async_computation.7 | async-start | bytes 393216 | tf_op jit(solution)/shard_map/all_to_all | solution.py:21
  228.8 8.4 %all-to-all-done.7 = bf16[32,24,128]{2,1,0:T(8,128)(2,1)S(1)} async-done(((bf16[32,24,128]{2,1,0:T(8,128)(2,1)}), bf16[32,24,128]{2,1,0:T(8,128)(2,1)S(1)}, u32[]{:S(2)}, u32[]{:S(2)}) %all-to-all-start.7) | async-done | bytes 196640 | tf_op jit(solution)/shard_map/all_to_all | solution.py:21
  237.2 0.1 reshape.175
  237.3 0.1 subtract_divide_fusion.1
  237.4 0.1 broadcast_multiply_fusion
  237.5 1.4 fusion.24
  (45 shorter events, 0.6 us)
Async XLA Ops:
  0.6 34.1 %copy-start = (bf16[1,1,96,128,128]{4,3,2,1,0:T(8,128)(2,1)S(1)}, bf16[1,1,96,128,128]{4,3,2,1,0:T(8,128)(2,1)}, u32[]{:S(2)}) copy-start(bf16[1,1,96,128,128]{4,3,2,1,0:T(8,128)(2,1)} %param.8) | copy-start | bytes 9437188
  0.6 3.8 %copy-start.2 = (s32[1,1,96]{2,1,0:T(1,128)S(1)}, s32[1,1,96]{2,1,0:T(1,128)}, u32[]{:S(2)}) copy-start(s32[1,1,96]{2,1,0:T(1,128)} %param.9) | copy-start | bytes 1156
  0.7 33.9 %copy-start.9 = (s32[256]{0:T(256)S(1)}, s32[256]{0:T(256)}, u32[]{:S(2)}) copy-start(s32[256]{0:T(256)} %param.6) | copy-start | bytes 3076
  0.7 34.0 %copy-start.3 = (s32[1,1,96]{2,1,0:T(1,128)S(1)}, s32[1,1,96]{2,1,0:T(1,128)}, u32[]{:S(2)}) copy-start(s32[1,1,96]{2,1,0:T(1,128)} %param.10) | copy-start | bytes 1156
  0.7 34.0 %copy-start.8 = (f32[256]{0:T(256)S(1)}, f32[256]{0:T(256)}, u32[]{:S(2)}) copy-start(f32[256]{0:T(256)} %param.7) | copy-start | bytes 3076
  5.3 51.3 %all-to-all-start = ((f32[32,2,128]{2,1,0:T(2,128)}), f32[32,2,128]{2,1,0:T(2,128)S(1)}, u32[]{:S(2)}, u32[]{:S(2)}) async-start(f32[32,2,128]{2,1,0:T(2,128)} %copy.8), calls=%async_computation | async-start | bytes 65536 | tf_op jit(solution)/shard_map/all_to_all | solution.py:21
  36.3 117.4 %copy-start.5 = (f32[2,8,128]{2,1,0:T(8,128)}, f32[2,8,128]{2,1,0:T(8,128)S(1)}, u32[]{:S(2)}) copy-start(f32[2,8,128]{2,1,0:T(8,128)S(1)} %fusion.29) | copy-start | bytes 24580
  57.7 22.2 %all-to-all-start.1 = ((bf16[32,80,128]{2,1,0:T(8,128)(2,1)}), bf16[32,80,128]{2,1,0:T(8,128)(2,1)}, u32[]{:S(2)}, u32[]{:S(2)}) async-start(bf16[32,80,128]{2,1,0:T(8,128)(2,1)} %broadcast_in_dim.57), calls=%async_computation.1 | async-start | bytes 1310720 | tf_op jit(solution)/shard_map/all_to_all | solution.py:21
  83.0 44.9 %copy-start.7 = (f32[2,1,128]{2,1,0:T(1,128)}, f32[2,1,128]{2,1,0:T(1,128)S(1)}, u32[]{:S(2)}) copy-start(f32[2,1,128]{2,1,0:T(1,128)S(1)} %constant_dynamic-slice_fusion) | copy-start | bytes 3076
  119.2 0.7 copy-start.4
  121.4 0.7 copy-start.1
  122.1 14.8 %all-to-all-start.3 = ((f32[32,16,128]{2,1,0:T(8,128)}), f32[32,16,128]{2,1,0:T(8,128)S(1)}, u32[]{:S(2)}, u32[]{:S(2)}) async-start(f32[32,16,128]{2,1,0:T(8,128)} %copy-done.1), calls=%async_computation.3 | async-start | bytes 524288 | tf_op jit(solution)/shard_map/all_to_all | solution.py:21
  149.0 34.0 %all-to-all-start.5 = ((bf16[32,16,128]{2,1,0:T(8,128)(2,1)}), bf16[32,16,128]{2,1,0:T(8,128)(2,1)S(1)}, u32[]{:S(2)}, u32[]{:S(2)}) async-start(bf16[32,16,128]{2,1,0:T(8,128)(2,1)} %get-tuple-element.28), calls=%async_computation.5 | async-start | bytes 262144 | tf_op jit(solution)/shard_map/all_to_all | solution.py:21
  183.2 54.3 %copy-start.6 = (f32[2,8,128]{2,1,0:T(8,128)S(1)}, f32[2,8,128]{2,1,0:T(8,128)}, u32[]{:S(2)}) copy-start(f32[2,8,128]{2,1,0:T(8,128)} %copy-done.5) | copy-start | bytes 24580
  184.8 32.7 %all-to-all-start.6 = ((bf16[32,2,1152]{2,1,0:T(2,128)(2,1)}), bf16[32,2,1152]{2,1,0:T(2,128)(2,1)}, u32[]{:S(2)}, u32[]{:S(2)}) async-start(bf16[32,2,1152]{2,1,0:T(2,128)(2,1)} %fusion.11), calls=%async_computation.6 | async-start | bytes 294912 | tf_op jit(solution)/shard_map/all_to_all | solution.py:21
  219.7 17.4 %all-to-all-start.7 = ((bf16[32,24,128]{2,1,0:T(8,128)(2,1)}), bf16[32,24,128]{2,1,0:T(8,128)(2,1)S(1)}, u32[]{:S(2)}, u32[]{:S(2)}) async-start(bf16[32,24,128]{2,1,0:T(8,128)(2,1)} %pad_maximum_fusion), calls=%async_computation.7 | async-start | bytes 393216 | tf_op jit(solution)/shard_map/all_to_all | solution.py:21

commit v6 on v5

--- a/solution.py
+++ b/solution.py
@@ -135,7 +135,8 @@
     classes_now = jnp.arange(CLASSES, dtype=jnp.int32)[:, None]
     labels = jnp.where(kinds[:, None] == classes_now, weight[:, None], jnp.float32(0.0))
     table = jnp.broadcast_to(classes_now.astype(BF16), (CLASSES, side))
-    known, labels, table, from_rows = lax.optimization_barrier((known, labels, table, from_rows))
+    place = lax.axis_index("clu").astype(jnp.uint32)
+    known, labels, table, place, from_rows = lax.optimization_barrier((known, labels, table, place, from_rows))
     sent = jnp.concatenate([known, split3(jnp.sum(from_rows, axis=0))])
     sent = jnp.pad(sent, ((0, -sent.shape[0] % 16), (0, 0)))
     got = swap(jnp.broadcast_to(sent[None], (n_clu,) + sent.shape), "clu")
@@ -145,9 +146,10 @@
         (shape((n_mem, height, side), BF16), shape((col_blocks, side), F32)),
         (row_space, col_space, (n_clu, got.shape[1] - col_blocks, side), (col_blocks, side)), LIMIT,
     )
-    inverse_root = lax.dynamic_index_in_dim(
-        col_root.reshape(NB_DEV, n_clu, side), lax.axis_index("clu"), 1, keepdims=False
-    )
+    none = jnp.zeros((), jnp.uint32)
+    inverse_root = lax.dynamic_slice(
+        col_root.reshape(NB_DEV, n_clu, side), (none, place, none), (NB_DEV, 1, side)
+    ).reshape(NB_DEV, side)
     own = jnp.concatenate([inverse_root * weight, kinds.astype(F32)], axis=1)
     peers = max(n_mem, n_clu)
     def panel_of(value, kind):

time: 240 us -> 238 us (level)
  blocking collectives: 47.4 us -> 69.3 us
  waiting for transfers between devices: 101 us -> 87.9 us
  starting transfers between devices: 61.8 us -> 52.7 us
    all_to_all x2 -> x3, blocking collectives: 47.4 us -> 69.3 us  [swap(): return lax.all_to_all(parts, axis, 0, 0, tiled=True)]
    all_to_all x6 -> x5, waiting for transfers between devices: 101 us -> 87.9 us  [swap(): return lax.all_to_all(parts, axis, 0, 0, tiled=True)]
    all_to_all x6 -> x5, starting transfers between devices: 61.8 us -> 52.7 us  [swap(): return lax.all_to_all(parts, axis, 0, 0, tiled=True)]
  transfers between devices with their start and end apart: 6 -> 5, of which waited for: 6 -> 5; matrix products, arithmetic and copies ran while one was open for 2% -> 2% of each run, Pallas kernels for 2% -> 2%
where the time goes in v6:
time: 238 us; the launch traced here: 237 us
  waiting for transfers between devices  87.9 us (37%)
  blocking collectives  69.3 us (29%)
  starting transfers between devices  52.7 us (22%)
  other arithmetic  11.3 us (5%)
  Pallas kernels  10.1 us (4%)
  local copies, waits for them, and re-layouts  3.92 us (2%)
    all_to_all x5, waiting for transfers between devices, swap(): return lax.all_to_all(parts, axis, 0, 0, tiled=True)  87.9 us
    all_to_all x3, blocking collectives, swap(): return lax.all_to_all(parts, axis, 0, 0, tiled=True)  69.3 us
    all_to_all x5, starting transfers between devices, swap(): return lax.all_to_all(parts, axis, 0, 0, tiled=True)  52.7 us
    pallas_call x5, Pallas kernels, call_on_tiles(): pl.pallas_call(kernel, in_specs=[smem] * len(index) + [vmem] * (len(panel...  9.39 us
  transfers between devices with their start and end apart: 5, of which 5 were waited for; matrix products, arithmetic and copies ran while one was open for 2% of the time, Pallas kernels for 2%

profile of v6, /device:TPU:1, one launch (start us, length us, event | category | flops | bytes accessed | tf_op | source)
XLA Modules:
  0.0 237.2 jit_solution(140316395020408378)
XLA Ops:
  0.6 0.0 copy-start
  0.6 0.0 copy-start.2
  0.7 0.0 copy-start.9
  0.7 0.0 copy-start.3
  0.7 0.0 copy-start.8
  1.5 2.9 %convert_reduce_fusion = f32[96,128]{1,0:T(8,128)S(1)} fusion(bf16[1,1,96,128,128]{4,3,2,1,0:T(8,128)(2,1)} %param.8), kind=kLoop, calls=%fused_computation | loop fusion | flops 3133440 | bytes 3194880 | tf_op jit(solution)/shard_map/reduce_sum | solution.py:123
  4.5 0.0 copy-done.2
  4.5 0.2 fusion
  4.7 0.6 copy.8
  5.3 29.3 %all-to-all-start = ((f32[32,2,128]{2,1,0:T(2,128)}), f32[32,2,128]{2,1,0:T(2,128)S(1)}, u32[]{:S(2)}, u32[]{:S(2)}) async-start(f32[32,2,128]{2,1,0:T(2,128)} %copy.8), calls=%async_computation | async-start | bytes 65536 | tf_op jit(solution)/shard_map/all_to_all | solution.py:21
  34.6 0.0 copy-done.9
  34.6 0.0 copy-done.3
  34.6 0.0 copy-done.8
  34.7 0.0 copy-done
  34.7 1.5 shard_map.77
  36.3 0.0 copy-start.5
  36.3 20.3 %all-to-all-done = f32[32,2,128]{2,1,0:T(2,128)S(1)} async-done(((f32[32,2,128]{2,1,0:T(2,128)}), f32[32,2,128]{2,1,0:T(2,128)S(1)}, u32[]{:S(2)}, u32[]{:S(2)}) %all-to-all-start) | async-done | bytes 32800 | tf_op jit(solution)/shard_map/all_to_all | solution.py:21
  56.6 0.1 broadcast_in_dim.56
  56.7 0.1 broadcast_in_dim.57
  56.8 21.9 %all_to_all.40.got = bf16[32,80,128]{2,1,0:T(8,128)(2,1)S(1)} all-to-all(bf16[32,80,128]{2,1,0:T(8,128)(2,1)S(1)} %broadcast_in_dim.57), channel_id=1, replica_groups=mesh['clu'=32,'mem'=32] {'clu'}, dimensions={0} | all-to-all | bytes 1310720 | tf_op jit(solution)/shard_map/all_to_all | solution.py:21
  78.7 2.5 %shard_map.78 = (bf16[32,16,128]{2,1,0:T(8,128)(2,1)S(1)}, f32[64,128]{1,0:T(8,128)S(1)}) custom-call(s32[96]{0:T(128)S(1)} %bitcast.100, s32[1]{0:T(128)} %bitcast.88.count_ref, s32[96]{0:T(128)S(1)} %fusion.36.into_ref.from_ref, bf16[32,80,128]{2,1,0:T(8,128)(2,1)S(1)} %all_to_all.40.got, bf16[96,128,128]{2,1,0:T(8,128)(2,1)S(1)} %bitcast.94), custom_call_target="tpu_custom_call" | custom-call | flops 25165824 | bytes 3145728 | tf_op jit(solution)/shard_map/pallas_call | solution.py:93
  81.3 0.0 copy-start.7
  81.4 0.1 pad_maximum_fusion.1
  81.6 35.9 %all_to_all.41 = bf16[32,2,1280]{2,1,0:T(2,128)(2,1)S(1)} all-to-all(bf16[32,2,1280]{2,1,0:T(2,128)(2,1)S(1)} %pad_maximum_fusion.1), channel_id=1, replica_groups=mesh['clu'=32,'mem'=32] {'mem'}, dimensions={0} | all-to-all | bytes 327680 | tf_op jit(solution)/shard_map/all_to_all | solution.py:21
  117.5 0.6 copy-done.4
  118.2 1.5 shard_map.79
  119.7 0.0 copy-start.1
  119.7 0.7 copy-done.1
  120.4 5.9 %all-to-all-start.3 = ((f32[32,16,128]{2,1,0:T(8,128)}), f32[32,16,128]{2,1,0:T(8,128)S(1)}, u32[]{:S(2)}, u32[]{:S(2)}) async-start(f32[32,16,128]{2,1,0:T(8,128)} %copy-done.1), calls=%async_computation.3 | async-start | bytes 524288 | tf_op jit(solution)/shard_map/all_to_all | solution.py:21
  126.4 1.1 convert_reduce_fusion.2
  127.4 7.8 %all-to-all-done.3.from_cols = f32[32,16,128]{2,1,0:T(8,128)S(1)} async-done(((f32[32,16,128]{2,1,0:T(8,128)}), f32[32,16,128]{2,1,0:T(8,128)S(1)}, u32[]{:S(2)}, u32[]{:S(2)}) %all-to-all-start.3) | async-done | bytes 262176 | tf_op jit(solution)/shard_map/all_to_all | solution.py:21
  135.2 0.7 shard_map.80
  135.9 11.5 %all_to_all.42.panel = bf16[32,16,128]{2,1,0:T(8,128)(2,1)S(1)} all-to-all(bf16[32,16,128]{2,1,0:T(8,128)(2,1)} %get-tuple-element.30), channel_id=1, replica_groups=mesh['clu'=32,'mem'=32] {'clu'}, dimensions={0} | all-to-all | bytes 262144 | tf_op jit(solution)/shard_map/all_to_all | solution.py:21
  147.4 3.9 %all-to-all-start.5 = ((bf16[32,16,128]{2,1,0:T(8,128)(2,1)}), bf16[32,16,128]{2,1,0:T(8,128)(2,1)S(1)}, u32[]{:S(2)}, u32[]{:S(2)}) async-start(bf16[32,16,128]{2,1,0:T(8,128)(2,1)} %get-tuple-element.30), calls=%async_computation.5 | async-start | bytes 262144 | tf_op jit(solution)/shard_map/all_to_all | solution.py:21
  151.3 0.5 iota_compare_fusion.2
  151.8 0.1 multiply_reduce_fusion.1
  151.9 0.1 reduce_sum.128
  152.0 0.1 multiply_reduce_fusion.2
  152.2 0.1 reduce-precision_convert_fusion.9
  152.3 0.1 fusion.38
  152.4 0.5 pad.26
  152.9 2.3 shard_map.81
  155.2 0.6 broadcast_in_dim.100
  155.8 0.8 pad_maximum_fusion.2
  156.6 24.8 %all-to-all-done.5.panel = bf16[32,16,128]{2,1,0:T(8,128)(2,1)S(1)} async-done(((bf16[32,16,128]{2,1,0:T(8,128)(2,1)}), bf16[32,16,128]{2,1,0:T(8,128)(2,1)S(1)}, u32[]{:S(2)}, u32[]{:S(2)}) %all-to-all-start.5) | async-done | bytes 131104 | tf_op jit(solution)/shard_map/all_to_all | solution.py:21
  181.4 0.2 multiply_reduce_fusion
  181.6 0.1 reduce_sum.131
  181.7 0.1 select_maximum_fusion.2
  181.7 1.4 fusion.11
  183.2 4.6 %all-to-all-start.6 = ((bf16[32,2,1152]{2,1,0:T(2,128)(2,1)}), bf16[32,2,1152]{2,1,0:T(2,128)(2,1)}, u32[]{:S(2)}, u32[]{:S(2)}) async-start(bf16[32,2,1152]{2,1,0:T(2,128)(2,1)} %fusion.11), calls=%async_computation.6 | async-start | bytes 294912 | tf_op jit(solution)/shard_map/all_to_all | solution.py:21
  187.7 1.5 shard_map.82
  189.3 26.6 %all-to-all-done.6 = bf16[32,2,1152]{2,1,0:T(2,128)(2,1)} async-done(((bf16[32,2,1152]{2,1,0:T(2,128)(2,1)}), bf16[32,2,1152]{2,1,0:T(2,128)(2,1)}, u32[]{:S(2)}, u32[]{:S(2)}) %all-to-all-start.6) | async-done | bytes 147488 | tf_op jit(solution)/shard_map/all_to_all | solution.py:21
  215.9 1.0 convert_reduce_fusion.3
  217.0 0.1 reshape.177
  217.1 0.1 reshape.176
  217.2 0.1 reduce-precision_convert_fusion.5
  217.3 0.1 fusion.37
  217.4 0.7 pad_maximum_fusion
  218.1 9.0 %all-to-all-start.7 = ((bf16[32,24,128]{2,1,0:T(8,128)(2,1)}), bf16[32,24,128]{2,1,0:T(8,128)(2,1)S(1)}, u32[]{:S(2)}, u32[]{:S(2)}) async-start(bf16[32,24,128]{2,1,0:T(8,128)(2,1)} %pad_maximum_fusion), calls=%async_computation.7 | async-start | bytes 393216 | tf_op jit(solution)/shard_map/all_to_all | solution.py:21
  227.2 8.4 %all-to-all-done.7 = bf16[32,24,128]{2,1,0:T(8,128)(2,1)S(1)} async-done(((bf16[32,24,128]{2,1,0:T(8,128)(2,1)}), bf16[32,24,128]{2,1,0:T(8,128)(2,1)S(1)}, u32[]{:S(2)}, u32[]{:S(2)}) %all-to-all-start.7) | async-done | bytes 196640 | tf_op jit(solution)/shard_map/all_to_all | solution.py:21
  235.6 0.1 reshape.179
  235.7 0.1 subtract_divide_fusion.1
  235.8 0.1 broadcast_multiply_fusion
  235.9 1.4 fusion.24
  (44 shorter events, 0.6 us)
Async XLA Ops:
  0.6 34.1 %copy-start = (bf16[1,1,96,128,128]{4,3,2,1,0:T(8,128)(2,1)S(1)}, bf16[1,1,96,128,128]{4,3,2,1,0:T(8,128)(2,1)}, u32[]{:S(2)}) copy-start(bf16[1,1,96,128,128]{4,3,2,1,0:T(8,128)(2,1)} %param.8) | copy-start | bytes 9437188
  0.6 3.8 %copy-start.2 = (s32[1,1,96]{2,1,0:T(1,128)S(1)}, s32[1,1,96]{2,1,0:T(1,128)}, u32[]{:S(2)}) copy-start(s32[1,1,96]{2,1,0:T(1,128)} %param.9) | copy-start | bytes 1156
  0.7 33.9 %copy-start.9 = (s32[256]{0:T(256)S(1)}, s32[256]{0:T(256)}, u32[]{:S(2)}) copy-start(s32[256]{0:T(256)} %param.6) | copy-start | bytes 3076
  0.7 34.0 %copy-start.3 = (s32[1,1,96]{2,1,0:T(1,128)S(1)}, s32[1,1,96]{2,1,0:T(1,128)}, u32[]{:S(2)}) copy-start(s32[1,1,96]{2,1,0:T(1,128)} %param.10) | copy-start | bytes 1156
  0.7 34.0 %copy-start.8 = (f32[256]{0:T(256)S(1)}, f32[256]{0:T(256)}, u32[]{:S(2)}) copy-start(f32[256]{0:T(256)} %param.7) | copy-start | bytes 3076
  5.3 51.3 %all-to-all-start = ((f32[32,2,128]{2,1,0:T(2,128)}), f32[32,2,128]{2,1,0:T(2,128)S(1)}, u32[]{:S(2)}, u32[]{:S(2)}) async-start(f32[32,2,128]{2,1,0:T(2,128)} %copy.8), calls=%async_computation | async-start | bytes 65536 | tf_op jit(solution)/shard_map/all_to_all | solution.py:21
  36.3 115.8 %copy-start.5 = (f32[2,8,128]{2,1,0:T(8,128)}, f32[2,8,128]{2,1,0:T(8,128)S(1)}, u32[]{:S(2)}) copy-start(f32[2,8,128]{2,1,0:T(8,128)S(1)} %fusion.29) | copy-start | bytes 24580
  81.3 45.1 %copy-start.7 = (f32[2,1,128]{2,1,0:T(1,128)}, f32[2,1,128]{2,1,0:T(1,128)S(1)}, u32[]{:S(2)}) copy-start(f32[2,1,128]{2,1,0:T(1,128)S(1)} %constant_dynamic-slice_fusion) | copy-start | bytes 3076
  117.5 0.7 copy-start.4
  119.7 0.7 copy-start.1
  120.4 14.9 %all-to-all-start.3 = ((f32[32,16,128]{2,1,0:T(8,128)}), f32[32,16,128]{2,1,0:T(8,128)S(1)}, u32[]{:S(2)}, u32[]{:S(2)}) async-start(f32[32,16,128]{2,1,0:T(8,128)} %copy-done.1), calls=%async_computation.3 | async-start | bytes 524288 | tf_op jit(solution)/shard_map/all_to_all | solution.py:21
  147.4 34.0 %all-to-all-start.5 = ((bf16[32,16,128]{2,1,0:T(8,128)(2,1)}), bf16[32,16,128]{2,1,0:T(8,128)(2,1)S(1)}, u32[]{:S(2)}, u32[]{:S(2)}) async-start(bf16[32,16,128]{2,1,0:T(8,128)(2,1)} %get-tuple-element.30), calls=%async_computation.5 | async-start | bytes 262144 | tf_op jit(solution)/shard_map/all_to_all | solution.py:21
  181.5 54.3 %copy-start.6 = (f32[2,8,128]{2,1,0:T(8,128)S(1)}, f32[2,8,128]{2,1,0:T(8,128)}, u32[]{:S(2)}) copy-start(f32[2,8,128]{2,1,0:T(8,128)} %copy-done.5) | copy-start | bytes 24580
  183.2 32.7 %all-to-all-start.6 = ((bf16[32,2,1152]{2,1,0:T(2,128)(2,1)}), bf16[32,2,1152]{2,1,0:T(2,128)(2,1)}, u32[]{:S(2)}, u32[]{:S(2)}) async-start(bf16[32,2,1152]{2,1,0:T(2,128)(2,1)} %fusion.11), calls=%async_computation.6 | async-start | bytes 294912 | tf_op jit(solution)/shard_map/all_to_all | solution.py:21
  218.1 17.4 %all-to-all-start.7 = ((bf16[32,24,128]{2,1,0:T(8,128)(2,1)}), bf16[32,24,128]{2,1,0:T(8,128)(2,1)S(1)}, u32[]{:S(2)}, u32[]{:S(2)}) async-start(bf16[32,24,128]{2,1,0:T(8,128)(2,1)} %pad_maximum_fusion), calls=%async_computation.7 | async-start | bytes 393216 | tf_op jit(solution)/shard_map/all_to_all | solution.py:21
